TPU v7x, 512 devices: a whole 4x4x16 slice. The times are simulated.
512 devices in a mesh: gx: 32 (over z, core), gy: 4 (over x), gz: 4 (over y).
Axes of the slice: x: 4, y: 4, z: 16, core: 2. Of those that a mesh axis runs over, the one named last changes fastest.
Arguments:
- positions: float32 [32, 4, 4, 3, 512], P('gx', 'gy', 'gz'), may hold values from 0 to 1.5
- species: int32 [32, 4, 4, 512], P('gx', 'gy', 'gz'), may hold values from 0 to 2
- plan: int32 [32, 4, 4, 4], P('gx', 'gy', 'gz'), may hold values from 0 to 2, as said below
- pair_centre: int32 [32, 4, 4, 512], P('gx', 'gy', 'gz'), may hold values from 0 to 767, as said below
- pair_neighbour: int32 [32, 4, 4, 512], P('gx', 'gy', 'gz'), may hold values from 0 to 20735, as said below
- pair_blocks: int32 [32, 4, 4], P('gx', 'gy', 'gz'), may hold values from 1 to 4
- w_in: bfloat16 [256, 14], replicated, may hold values from -1.5 to 1.5
- w_hidden: bfloat16 [256, 256], replicated, may hold values from -0.375 to 0.375
- w_env: bfloat16 [2, 64, 256], replicated, may hold values from -0.375 to 0.375
- w_latent: bfloat16 [2, 256, 320], replicated, may hold values from -0.3125 to 0.3125
- w_out: bfloat16 [256], replicated, may hold values from -0.375 to 0.375
Outputs:
- forces: float32 [32, 4, 4, 3, 768], P('gx', 'gy', 'gz')
- domain_energy: float32 [32, 4, 4], P('gx', 'gy', 'gz')
Inputs may be any that keep to these rules, and one draw needn't show every extreme that they name: Each domain sends at most 1 block with plan 1 and at most 1 with plan 2; some domain sends 1 each way. `pair_centre`: live pairs name slots of the layout that hold an atom; padded pairs may name any slot. `pair_neighbour`: live pairs name a slot of the extended array that holds an atom and is not the pair's centre; padded pairs may name any slot.
All inputs are finite; a program needn't handle non-finite values.
Results may differ from a plain program's by a relative error of at most 0.039.
Values sent between devices are 32-bit elements; how exact they have to be, the bound alone decides.
A program may use at most 64 MiB of HBM per device.

v0:
```python
import jax
import jax.numpy as jnp
from jax import lax
from jax.sharding import PartitionSpec as P

MULT = 64
NBASIS = 8
NSPEC = 3
LAYERS = 2
PAIR_BLK = 128
CAP = 1


edge_length = 1.5
cutoff = 9.0
softening = 0.5
env_scale = 0.5


def passed_along(value, axis, steps):
    count = lax.axis_size(axis)
    pairs = [(source, (source + steps) % count) for source in range(count)]
    return lax.ppermute(value, axis, pairs)


def with_halo(shard, sides, width):
    for axis, dim in sides:
        peers, length = (lax.axis_size(axis), shard.shape[dim])
        up = [(i, (i + 1) % peers) for i in range(peers)]
        down = [(j, i) for i, j in up]
        last = lax.slice_in_dim(shard, length - width, length, axis=dim)
        first = lax.slice_in_dim(shard, 0, width, axis=dim)
        before = lax.ppermute(last, axis, up)
        after = lax.ppermute(first, axis, down)
        shard = jnp.concatenate([before, shard, after], axis=dim)
    return shard


def offset_table():
    offset_ids = jnp.arange(27)
    return jnp.stack([offset_ids // 9 - 1, offset_ids // 3 % 3 - 1, offset_ids % 3 - 1], 1).astype(
        jnp.float32
    )


def pack_blocks(block_data, chosen_mask, x_shift):
    chosen = chosen_mask.astype(jnp.int32)
    ranking = jnp.cumsum(chosen, axis=-1) - 1
    slot_ids = jnp.arange(CAP, dtype=jnp.int32)
    chosen_slots = (
        (ranking[..., None, :] == slot_ids[:, None]) & (chosen[..., None, :] == 1)
    ).astype(jnp.float32)
    packed = jnp.einsum(
        "...kb,...bcs->...kcs", chosen_slots, block_data, precision=lax.Precision.HIGHEST
    )
    filled = jnp.sum(chosen_slots, -1)
    first_channel = (jnp.arange(4) == 0).astype(jnp.float32)
    return packed + x_shift * filled[..., :, None, None] * first_channel[:, None]


def pair_energy(
    ext_pos, ext_kind, centre, neighbour, live_pairs, w_in, w_hidden, w_env, w_latent, w_out
):
    slot_count = ext_pos.shape[2]
    pair_total = centre.shape[0]
    flat_pos = jnp.transpose(ext_pos, (1, 0, 2)).reshape(3, 27 * slot_count)
    flat_kind = ext_kind.reshape(27 * slot_count)
    centre_ext = centre + 13 * slot_count
    displacement = flat_pos[:, neighbour] - flat_pos[:, centre_ext]
    distance = jnp.sqrt(jnp.sum(displacement * displacement, 0) + softening * softening)
    direction = displacement / distance[None]
    scaled = distance / cutoff
    envelope = (1.0 - scaled * scaled) ** 2
    basis_orders = jnp.arange(1, NBASIS + 1).astype(jnp.float32)
    radial_basis = (
        jnp.sin(basis_orders[:, None] * jnp.pi * scaled[None]) / distance[None] * envelope[None]
    )
    species_ids = jnp.arange(NSPEC).astype(jnp.float32)
    centre_hot = (flat_kind[centre_ext][None] == species_ids[:, None]).astype(jnp.float32)
    neighbour_hot = (flat_kind[neighbour][None] == species_ids[:, None]).astype(jnp.float32)
    features = jnp.concatenate([radial_basis, centre_hot, neighbour_hot], 0).astype(jnp.bfloat16)
    first_hidden = jax.nn.silu(jnp.dot(w_in, features, preferred_element_type=jnp.float32)).astype(
        jnp.bfloat16
    )
    latent = (
        jax.nn.silu(jnp.dot(w_hidden, first_hidden, preferred_element_type=jnp.float32))
        * envelope[None]
    )
    harmonics = jnp.concatenate([jnp.ones((1, pair_total), jnp.float32), direction], 0)
    for layer_index in range(LAYERS):
        latent_half = latent.astype(jnp.bfloat16)
        env_weights = (
            jnp.dot(w_env[layer_index], latent_half, preferred_element_type=jnp.float32)
            * live_pairs[None]
        )
        env_terms = (harmonics[:, None, :] * env_weights[None]).reshape(4 * MULT, pair_total)
        environment = jnp.zeros((4 * MULT, slot_count), jnp.float32).at[:, centre].add(env_terms)
        centre_env = environment[:, centre].reshape(4, MULT, pair_total)
        invariant = (
            env_scale * env_weights * jnp.sum(harmonics[:, None, :] * centre_env, 0)
        ).astype(jnp.bfloat16)
        combined = jnp.concatenate([latent_half, invariant], 0)
        latent = latent + jax.nn.silu(
            jnp.dot(w_latent[layer_index], combined, preferred_element_type=jnp.float32)
        )
    pair_values = jnp.dot(w_out, latent.astype(jnp.bfloat16), preferred_element_type=jnp.float32)
    return jnp.sum(pair_values * live_pairs)


def on_device(
    positions,
    species,
    plan,
    pair_centre,
    pair_neighbour,
    pair_blocks,
    w_in,
    w_hidden,
    w_env,
    w_latent,
    w_out,
):
    atom_total = positions.shape[4]
    block_count = plan.shape[3]
    block_size = atom_total // block_count
    coords = positions.reshape(3, block_count, block_size).transpose(1, 0, 2)
    kind_rows = (species.astype(jnp.float32) + 1.0).reshape(block_count, 1, block_size)
    block_data = jnp.concatenate([coords, kind_rows], 1)
    block_moves = plan.reshape(block_count)
    packed_up = pack_blocks(block_data, block_moves == 1, -edge_length)
    packed_down = pack_blocks(block_data, block_moves == 2, edge_length)
    staying = (block_moves == 0).astype(jnp.float32)[:, None, None] * block_data
    from_lower = passed_along(packed_up, "gx", 1)
    from_upper = passed_along(packed_down, "gx", -1)
    arranged = jnp.concatenate([from_lower, staying, from_upper], 0)
    slot_count = arranged.shape[0] * block_size
    layout = arranged.transpose(1, 0, 2).reshape(1, 1, 1, 4, slot_count)
    extended = with_halo(layout, (("gx", 0), ("gy", 1), ("gz", 2)), 1).reshape(27, 4, slot_count)
    ext_pos = extended[:, :3] + edge_length * offset_table()[:, :, None]
    ext_kind = extended[:, 3] - 1.0
    pair_total = pair_centre.shape[3]
    live_pairs = (jnp.arange(pair_total) < pair_blocks.reshape(()) * PAIR_BLK).astype(jnp.float32)
    centre = pair_centre.reshape(pair_total)
    neighbour = pair_neighbour.reshape(pair_total)

    def energy_of(field_pos):
        return pair_energy(
            field_pos,
            ext_kind,
            centre,
            neighbour,
            live_pairs,
            w_in,
            w_hidden,
            w_env,
            w_latent,
            w_out,
        )

    energy, pullback = jax.vjp(energy_of, ext_pos)
    partial_value = -pullback(jnp.ones((), jnp.float32))[0]
    totals = partial_value[13]
    for offset_index in range(27):
        shift_x = offset_index // 9 - 1
        shift_y = offset_index // 3 % 3 - 1
        shift_z = offset_index % 3 - 1
        if offset_index != 13:
            moved = partial_value[offset_index]
            if shift_x != 0:
                moved = passed_along(moved, "gx", shift_x)
            if shift_y != 0:
                moved = passed_along(moved, "gy", shift_y)
            if shift_z != 0:
                moved = passed_along(moved, "gz", shift_z)
            totals = totals + moved
    return (totals.reshape(1, 1, 1, 3, slot_count), energy.reshape(1, 1, 1))


def solution(mesh):
    return jax.shard_map(
        on_device,
        mesh=mesh,
        in_specs=(
            P("gx", "gy", "gz", None, None),
            P("gx", "gy", "gz", None),
            P("gx", "gy", "gz", None),
            P("gx", "gy", "gz", None),
            P("gx", "gy", "gz", None),
            P("gx", "gy", "gz"),
            P(),
            P(),
            P(),
            P(),
            P(),
        ),
        out_specs=(P("gx", "gy", "gz", None, None), P("gx", "gy", "gz")),
        check_vma=False,
    )
```

profile of v0, /device:TPU:6, one launch (start us, length us, event | category | flops | bytes accessed | tf_op | source)
XLA Modules:
  0.0 285.9 jit_solution(7258616554258947374)
XLA Ops:
  6.8 8.9 %collective-permute-start.1 = (f32[1,4,128]{2,0,1:T(1,128)S(1)}, f32[1,4,128]{2,0,1:T(1,128)S(1)}, u32[]{:S(2)}, u32[]{:S(2)}) collective-permute-start(f32[1,4,128]{2,0,1:T(1,128)S(1)} %bitcast.331), channel_id=1, source_target_pairs={{0,496},{16,0},{32,16},{48,32},{64,48},{80,64},{96,80},{112,96},{1... | collective-permute-start | bytes 6152 | tf_op jit(solution)/shard_map/ppermute | solution.py:23
  19.8 3.0 %collective-permute-start.3 = (f32[1,1,1,4,768]{4,3,2,1,0:T(4,128)S(1)}, f32[1,1,1,4,768]{4,3,2,1,0:T(4,128)S(1)}, u32[]{:S(2)}, u32[]{:S(2)}) collective-permute-start(f32[1,1,1,4,768]{4,3,2,1,0:T(4,128)S(1)} %reshape.567), channel_id=1, source_target_pairs={{16,0},{32,16},{48,32},{64,48},{80,64},{96,80},{112,96},{128,112},... | collective-permute-start | bytes 36872 | tf_op jit(solution)/shard_map/ppermute | solution.py:34
  24.2 2.7 collective-permute-start.5
  26.9 4.3 %collective-permute-start.4 = (f32[3,1,1,4,768]{4,3,2,1,0:T(4,128)S(1)}, f32[3,1,1,4,768]{4,3,2,1,0:T(4,128)S(1)}, u32[]{:S(2)}, u32[]{:S(2)}) collective-permute-start(f32[3,1,1,4,768]{4,3,2,1,0:T(4,128)S(1)} %constant_dynamic-update-slice_fusion), channel_id=1, source_target_pairs={{0,4},{4,8},{8,12},{12,0},{1,5},{5,9},{9,13},{13,1},{2,6},{6,10},{... | collective-permute-start | bytes 110600 | tf_op jit(solution)/shard_map/ppermute | solution.py:33
  32.9 4.9 %collective-permute-start.7 = (f32[3,3,1,4,768]{4,3,2,1,0:T(4,128)S(1)}, f32[3,3,1,4,768]{4,3,2,1,0:T(4,128)S(1)}, u32[]{:S(2)}, u32[]{:S(2)}) collective-permute-start(f32[3,3,1,4,768]{4,3,2,1,0:T(4,128)S(1)} %pad_maximum_fusion.1), channel_id=1, source_target_pairs={{1,0},{2,1},{3,2},{0,3},{5,4},{6,5},{7,6},{4,7},{9,8},{10,9},{11,1... | collective-permute-start | bytes 331784 | tf_op jit(solution)/shard_map/ppermute | solution.py:34
  40.1 5.5 %collective-permute-done.6 = f32[3,3,1,4,768]{4,3,2,1,0:T(4,128)S(1)} collective-permute-done((f32[3,3,1,4,768]{4,3,2,1,0:T(4,128)S(1)}, f32[3,3,1,4,768]{4,3,2,1,0:T(4,128)S(1)}, u32[]{:S(2)}, u32[]{:S(2)}) %collective-permute-start.6) | collective-permute-done | bytes 110624 | tf_op jit(solution)/shard_map/ppermute | solution.py:33
  45.9 3.1 %gather_fusion.3 = f32[512]{0:T(512)S(1)} fusion(f32[20736]{0:T(1024)S(1)} %sub.65, s32[1024]{0:T(1024)S(1)} %pad_clamp_fusion.2), kind=kCustom, calls=%fused_computation.3 | custom fusion | bytes 6144 | tf_op jit(solution)/shard_map/jvp()/gather | solution.py:80
  49.1 3.1 %gather_fusion.2 = f32[512]{0:T(512)S(1)} fusion(f32[20736]{0:T(1024)S(1)} %sub.65, s32[1024]{0:T(1024)S(1)} %pad_clamp_fusion.1), kind=kCustom, calls=%fused_computation.2 | custom fusion | bytes 6144 | tf_op jit(solution)/shard_map/jvp()/gather | solution.py:79
  52.2 5.6 %copy.111 = f32[27,3,768]{1,2,0:T(8,128)} copy(f32[27,3,768]{2,1,0:T(4,128)S(1)} %bitcast.310) | data formatting | bytes 497664
  57.8 9.4 %broadcast_add_fusion = f32[27,3,768]{1,2,0:T(8,128)} fusion(f32[27,3,768]{1,2,0:T(8,128)} %copy.111, f32[27,3]{1,0:T(8,128)S(1)} %copy.91), kind=kLoop, calls=%fused_computation.13 | loop fusion | flops 62208 | bytes 497988 | tf_op jit(solution)/shard_map/add | solution.py:139
  67.2 5.1 %gather_fusion.1 = f32[512,3]{1,0:T(8,128)S(1)} fusion(f32[3,20736]{0,1:T(8,128)} %bitcast.295, s32[1024]{0:T(1024)S(1)} %pad_clamp_fusion.1), kind=kCustom, calls=%fused_computation.1 | custom fusion | bytes 14336 | tf_op jit(solution)/shard_map/jvp()/gather | solution.py:69
  72.3 5.0 %gather_fusion = f32[512,3]{1,0:T(8,128)S(1)} fusion(f32[3,20736]{0,1:T(8,128)} %bitcast.296, s32[1024]{0:T(1024)S(1)} %pad_clamp_fusion.2), kind=kCustom, calls=%fused_computation | custom fusion | bytes 14336 | tf_op jit(solution)/shard_map/jvp()/gather | solution.py:69
  80.4 3.5 %scatter_custom_fusion = f32[256,768]{0,1:T(8,128)S(1)} fusion(s32[512]{0:T(512)S(1)} %bitcast.318, f32[512,256]{1,0:T(8,128)S(1)} %copy.96, f32[]{:T(128)} %constant.42.clone.1), kind=kCustom, calls=%fused_computation.90 | custom fusion | flops 131072 | bytes 786436 | tf_op jit(solution)/shard_map/jvp()/scatter-add | solution.py:97
  85.8 2.2 fusion.184
  88.5 3.8 %scatter_custom_fusion.1 = f32[256,768]{0,1:T(8,128)S(1)} fusion(s32[512]{0:T(512)} %bitcast.319, f32[512,256]{1,0:T(8,128)S(1)} %copy.98, f32[]{:T(128)} %constant.42.clone.1), kind=kCustom, calls=%fused_computation.88 | custom fusion | flops 131072 | bytes 786944 | tf_op jit(solution)/shard_map/jvp()/scatter-add | solution.py:97
  98.5 3.6 %scatter_custom_fusion.2 = f32[256,768]{0,1:T(8,128)S(1)} fusion(s32[512]{0:T(512)} %bitcast.320, f32[512,256]{1,0:T(8,128)S(1)} %copy.101, f32[]{:T(128)} %constant.42.clone.1), kind=kCustom, calls=%fused_computation.86 | custom fusion | flops 131072 | bytes 786944 | tf_op jit(solution)/shard_map/transpose(jvp())/scatter-add | solution.py:98
  108.5 3.8 %scatter_custom_fusion.3 = f32[256,768]{0,1:T(8,128)S(1)} fusion(s32[512]{0:T(512)} %bitcast.321, f32[512,256]{1,0:T(8,128)S(1)} %copy.103, f32[]{:T(128)} %constant.42.clone.1), kind=kCustom, calls=%fused_computation.84 | custom fusion | flops 131072 | bytes 786944 | tf_op jit(solution)/shard_map/transpose(jvp())/scatter-add | solution.py:98
  121.7 10.9 %scatter_custom_fusion.4 = f32[3,20736]{0,1:T(8,128)} fusion(s32[1024]{0:T(1024)} %bitcast.328, f32[1024,3]{1,0:T(8,128)S(1)} %copy.106, f32[]{:T(128)} %constant.42.clone.1), kind=kCustom, calls=%fused_computation.14 | custom fusion | flops 3072 | bytes 249344 | tf_op jit(solution)/shard_map/transpose(jvp())/add_any | solution.py:69
  132.6 9.0 %neg.48 = f32[3,20736]{0,1:T(8,128)} negate(f32[3,20736]{0,1:T(8,128)} %scatter_custom_fusion.4) | non-fusion elementwise | flops 62208 | bytes 497664 | tf_op jit(solution)/shard_map/neg | solution.py:161
  141.6 6.2 %copy.107 = f32[3,27,768]{2,0,1:T(4,128)S(1)} copy(f32[3,27,768]{0,2,1:T(8,128)} %bitcast.294) | data formatting | bytes 497664 | tf_op jit(solution)/shard_map/neg | solution.py:161
  151.1 2.9 %collective-permute-start.16 = (f32[3,768]{1,0:T(4,128)S(1)}, f32[3,768]{1,0:T(4,128)S(1)}, u32[]{:S(2)}, u32[]{:S(2)}) collective-permute-start(f32[3,768]{1,0:T(4,128)S(1)} %get-tuple-element.40), channel_id=1, source_target_pairs={{0,496},{16,0},{32,16},{48,32},{64,48},{80,64},{96,80},{112,96},{1... | collective-permute-start | bytes 27656 | tf_op jit(solution)/shard_map/ppermute | solution.py:23
  160.9 5.2 %collective-permute-start.39 = (f32[3,768]{1,0:T(4,128)S(1)}, f32[3,768]{1,0:T(4,128)S(1)}, u32[]{:S(2)}, u32[]{:S(2)}) collective-permute-start(f32[3,768]{1,0:T(4,128)S(1)} %get-tuple-element.26), channel_id=1, source_target_pairs={{0,4},{4,8},{8,12},{12,0},{1,5},{5,9},{9,13},{13,1},{2,6},{6,10},{... | collective-permute-start | bytes 27656 | tf_op jit(solution)/shard_map/ppermute | solution.py:23
  166.1 2.9 %collective-permute-start.38 = (f32[3,768]{1,0:T(4,128)S(1)}, f32[3,768]{1,0:T(4,128)S(1)}, u32[]{:S(2)}, u32[]{:S(2)}) collective-permute-start(f32[3,768]{1,0:T(4,128)S(1)} %get-tuple-element.27), channel_id=1, source_target_pairs={{0,4},{4,8},{8,12},{12,0},{1,5},{5,9},{9,13},{13,1},{2,6},{6,10},{... | collective-permute-start | bytes 27656 | tf_op jit(solution)/shard_map/ppermute | solution.py:23
  169.1 1.9 collective-permute-start.36
  173.0 5.1 %collective-permute-start.34 = (f32[3,768]{1,0:T(4,128)S(1)}, f32[3,768]{1,0:T(4,128)S(1)}, u32[]{:S(2)}, u32[]{:S(2)}) collective-permute-start(f32[3,768]{1,0:T(4,128)S(1)} %get-tuple-element.30), channel_id=1, source_target_pairs={{0,3},{1,0},{2,1},{3,2},{4,7},{5,4},{6,5},{7,6},{8,11},{9,8},{10,9... | collective-permute-start | bytes 27656 | tf_op jit(solution)/shard_map/ppermute | solution.py:23
  178.1 3.9 %collective-permute-start.32 = (f32[3,768]{1,0:T(4,128)S(1)}, f32[3,768]{1,0:T(4,128)S(1)}, u32[]{:S(2)}, u32[]{:S(2)}) collective-permute-start(f32[3,768]{1,0:T(4,128)S(1)} %get-tuple-element.31), channel_id=1, source_target_pairs={{0,12},{4,0},{8,4},{12,8},{1,13},{5,1},{9,5},{13,9},{2,14},{6,2},{... | collective-permute-start | bytes 27656 | tf_op jit(solution)/shard_map/ppermute | solution.py:23
  182.0 2.9 %collective-permute-start.31 = (f32[3,768]{1,0:T(4,128)S(1)}, f32[3,768]{1,0:T(4,128)S(1)}, u32[]{:S(2)}, u32[]{:S(2)}) collective-permute-start(f32[3,768]{1,0:T(4,128)S(1)} %get-tuple-element.32), channel_id=1, source_target_pairs={{0,12},{4,0},{8,4},{12,8},{1,13},{5,1},{9,5},{13,9},{2,14},{6,2},{... | collective-permute-start | bytes 27656 | tf_op jit(solution)/shard_map/ppermute | solution.py:23
  187.4 3.1 %collective-permute-start.12 = (f32[3,768]{1,0:T(4,128)S(1)}, f32[3,768]{1,0:T(4,128)S(1)}, u32[]{:S(2)}, u32[]{:S(2)}) collective-permute-start(f32[3,768]{1,0:T(4,128)S(1)} %collective-permute-done.11), channel_id=1, source_target_pairs={{0,12},{4,0},{8,4},{12,8},{1,13},{5,1},{9,5},{13,9},{2,14},{6,2},{... | collective-permute-start | bytes 27656 | tf_op jit(solution)/shard_map/ppermute | solution.py:23
  190.5 3.9 %collective-permute-start.25 = (f32[3,768]{1,0:T(4,128)S(1)}, f32[3,768]{1,0:T(4,128)S(1)}, u32[]{:S(2)}, u32[]{:S(2)}) collective-permute-start(f32[3,768]{1,0:T(4,128)S(1)} %collective-permute-done.24), channel_id=1, source_target_pairs={{0,4},{4,8},{8,12},{12,0},{1,5},{5,9},{9,13},{13,1},{2,6},{6,10},{... | collective-permute-start | bytes 27656 | tf_op jit(solution)/shard_map/ppermute | solution.py:23
  194.5 3.6 %collective-permute-start.22 = (f32[3,768]{1,0:T(4,128)S(1)}, f32[3,768]{1,0:T(4,128)S(1)}, u32[]{:S(2)}, u32[]{:S(2)}) collective-permute-start(f32[3,768]{1,0:T(4,128)S(1)} %collective-permute-done.21), channel_id=1, source_target_pairs={{0,4},{4,8},{8,12},{12,0},{1,5},{5,9},{9,13},{13,1},{2,6},{6,10},{... | collective-permute-start | bytes 27656 | tf_op jit(solution)/shard_map/ppermute | solution.py:23
  200.1 5.1 %collective-permute-start.17 = (f32[3,768]{1,0:T(4,128)S(1)}, f32[3,768]{1,0:T(4,128)S(1)}, u32[]{:S(2)}, u32[]{:S(2)}) collective-permute-start(f32[3,768]{1,0:T(4,128)S(1)} %collective-permute-done.16), channel_id=1, source_target_pairs={{0,3},{1,0},{2,1},{3,2},{4,7},{5,4},{6,5},{7,6},{8,11},{9,8},{10,9... | collective-permute-start | bytes 27656 | tf_op jit(solution)/shard_map/ppermute | solution.py:23
  205.2 2.2 collective-permute-start.14
  207.4 1.9 collective-permute-start.9
  209.4 5.1 %collective-permute-start.60 = (f32[3,768]{1,0:T(4,128)S(1)}, f32[3,768]{1,0:T(4,128)S(1)}, u32[]{:S(2)}, u32[]{:S(2)}) collective-permute-start(f32[3,768]{1,0:T(4,128)S(1)} %collective-permute-done.59), channel_id=1, source_target_pairs={{0,4},{4,8},{8,12},{12,0},{1,5},{5,9},{9,13},{13,1},{2,6},{6,10},{... | collective-permute-start | bytes 27656 | tf_op jit(solution)/shard_map/ppermute | solution.py:23
  214.5 3.6 %collective-permute-start.58 = (f32[3,768]{1,0:T(4,128)S(1)}, f32[3,768]{1,0:T(4,128)S(1)}, u32[]{:S(2)}, u32[]{:S(2)}) collective-permute-start(f32[3,768]{1,0:T(4,128)S(1)} %collective-permute-done.57), channel_id=1, source_target_pairs={{0,4},{4,8},{8,12},{12,0},{1,5},{5,9},{9,13},{13,1},{2,6},{6,10},{... | collective-permute-start | bytes 27656 | tf_op jit(solution)/shard_map/ppermute | solution.py:23
  222.1 5.1 %collective-permute-start.50 = (f32[3,768]{1,0:T(4,128)S(1)}, f32[3,768]{1,0:T(4,128)S(1)}, u32[]{:S(2)}, u32[]{:S(2)}) collective-permute-start(f32[3,768]{1,0:T(4,128)S(1)} %collective-permute-done.49), channel_id=1, source_target_pairs={{0,3},{1,0},{2,1},{3,2},{4,7},{5,4},{6,5},{7,6},{8,11},{9,8},{10,9... | collective-permute-start | bytes 27656 | tf_op jit(solution)/shard_map/ppermute | solution.py:23
  227.2 3.9 %collective-permute-start.47 = (f32[3,768]{1,0:T(4,128)S(1)}, f32[3,768]{1,0:T(4,128)S(1)}, u32[]{:S(2)}, u32[]{:S(2)}) collective-permute-start(f32[3,768]{1,0:T(4,128)S(1)} %collective-permute-done.46), channel_id=1, source_target_pairs={{0,12},{4,0},{8,4},{12,8},{1,13},{5,1},{9,5},{13,9},{2,14},{6,2},{... | collective-permute-start | bytes 27656 | tf_op jit(solution)/shard_map/ppermute | solution.py:23
  231.2 2.2 collective-permute-start.45
  237.3 5.1 %collective-permute-start.37 = (f32[3,768]{1,0:T(4,128)S(1)}, f32[3,768]{1,0:T(4,128)S(1)}, u32[]{:S(2)}, u32[]{:S(2)}) collective-permute-start(f32[3,768]{1,0:T(4,128)S(1)} %collective-permute-done.36), channel_id=1, source_target_pairs={{0,3},{1,0},{2,1},{3,2},{4,7},{5,4},{6,5},{7,6},{8,11},{9,8},{10,9... | collective-permute-start | bytes 27656 | tf_op jit(solution)/shard_map/ppermute | solution.py:23
  244.4 5.1 %collective-permute-start.30 = (f32[3,768]{1,0:T(4,128)S(1)}, f32[3,768]{1,0:T(4,128)S(1)}, u32[]{:S(2)}, u32[]{:S(2)}) collective-permute-start(f32[3,768]{1,0:T(4,128)S(1)} %collective-permute-done.29), channel_id=1, source_target_pairs={{0,3},{1,0},{2,1},{3,2},{4,7},{5,4},{6,5},{7,6},{8,11},{9,8},{10,9... | collective-permute-start | bytes 27656 | tf_op jit(solution)/shard_map/ppermute | solution.py:23
  249.5 5.1 %collective-permute-start.27 = (f32[3,768]{1,0:T(4,128)S(1)}, f32[3,768]{1,0:T(4,128)S(1)}, u32[]{:S(2)}, u32[]{:S(2)}) collective-permute-start(f32[3,768]{1,0:T(4,128)S(1)} %collective-permute-done.26), channel_id=1, source_target_pairs={{0,4},{4,8},{8,12},{12,0},{1,5},{5,9},{9,13},{13,1},{2,6},{6,10},{... | collective-permute-start | bytes 27656 | tf_op jit(solution)/shard_map/ppermute | solution.py:23
  256.6 3.9 %collective-permute-start.15 = (f32[3,768]{1,0:T(4,128)S(1)}, f32[3,768]{1,0:T(4,128)S(1)}, u32[]{:S(2)}, u32[]{:S(2)}) collective-permute-start(f32[3,768]{1,0:T(4,128)S(1)} %collective-permute-done.14), channel_id=1, source_target_pairs={{0,1},{1,2},{2,3},{3,0},{4,5},{5,6},{6,7},{7,4},{8,9},{9,10},{10,1... | collective-permute-start | bytes 27656 | tf_op jit(solution)/shard_map/ppermute | solution.py:23
  260.5 3.1 %collective-permute-start.10 = (f32[3,768]{1,0:T(4,128)S(1)}, f32[3,768]{1,0:T(4,128)S(1)}, u32[]{:S(2)}, u32[]{:S(2)}) collective-permute-start(f32[3,768]{1,0:T(4,128)S(1)} %collective-permute-done.9), channel_id=1, source_target_pairs={{0,3},{1,0},{2,1},{3,2},{4,7},{5,4},{6,5},{7,6},{8,11},{9,8},{10,9... | collective-permute-start | bytes 27656 | tf_op jit(solution)/shard_map/ppermute | solution.py:23
  264.3 2.7 collective-permute-start.61
  267.0 4.3 %collective-permute-start.56 = (f32[3,768]{1,0:T(4,128)S(1)}, f32[3,768]{1,0:T(4,128)S(1)}, u32[]{:S(2)}, u32[]{:S(2)}) collective-permute-start(f32[3,768]{1,0:T(4,128)S(1)} %collective-permute-done.55), channel_id=1, source_target_pairs={{0,3},{1,0},{2,1},{3,2},{4,7},{5,4},{6,5},{7,6},{8,11},{9,8},{10,9... | collective-permute-start | bytes 27656 | tf_op jit(solution)/shard_map/ppermute | solution.py:23
  271.3 1.9 collective-permute-start.48
  273.3 5.1 %collective-permute-start.43 = (f32[3,768]{1,0:T(4,128)S(1)}, f32[3,768]{1,0:T(4,128)S(1)}, u32[]{:S(2)}, u32[]{:S(2)}) collective-permute-start(f32[3,768]{1,0:T(4,128)S(1)} %collective-permute-done.42), channel_id=1, source_target_pairs={{0,3},{1,0},{2,1},{3,2},{4,7},{5,4},{6,5},{7,6},{8,11},{9,8},{10,9... | collective-permute-start | bytes 27656 | tf_op jit(solution)/shard_map/ppermute | solution.py:23
  281.0 4.2 %collective-permute-done.28 = f32[3,768]{1,0:T(4,128)S(1)} collective-permute-done((f32[3,768]{1,0:T(4,128)S(1)}, f32[3,768]{1,0:T(4,128)S(1)}, u32[]{:S(2)}, u32[]{:S(2)}) %collective-permute-start.28) | collective-permute-done | bytes 9248 | tf_op jit(solution)/shard_map/ppermute | solution.py:23
  (225 shorter events, 72.3 us)
Async XLA Ops:
  5.2 14.5 %collective-permute-start = (f32[1,4,128]{2,0,1:T(1,128)S(1)}, f32[1,4,128]{2,0,1:T(1,128)S(1)}, u32[]{:S(2)}, u32[]{:S(2)}) collective-permute-start(f32[1,4,128]{2,0,1:T(1,128)S(1)} %bitcast.330), channel_id=1, source_target_pairs={{0,16},{16,32},{32,48},{48,64},{64,80},{80,96},{96,112},{112,128},... | collective-permute-start | bytes 6152 | tf_op jit(solution)/shard_map/ppermute | solution.py:23
  6.8 12.9 %collective-permute-start.1 = (f32[1,4,128]{2,0,1:T(1,128)S(1)}, f32[1,4,128]{2,0,1:T(1,128)S(1)}, u32[]{:S(2)}, u32[]{:S(2)}) collective-permute-start(f32[1,4,128]{2,0,1:T(1,128)S(1)} %bitcast.331), channel_id=1, source_target_pairs={{0,496},{16,0},{32,16},{48,32},{64,48},{80,64},{96,80},{112,96},{1... | collective-permute-start | bytes 6152 | tf_op jit(solution)/shard_map/ppermute | solution.py:23
  24.2 8.4 %collective-permute-start.5 = (f32[3,1,1,4,768]{4,3,2,1,0:T(4,128)S(1)}, f32[3,1,1,4,768]{4,3,2,1,0:T(4,128)S(1)}, u32[]{:S(2)}, u32[]{:S(2)}) collective-permute-start(f32[3,1,1,4,768]{4,3,2,1,0:T(4,128)S(1)} %constant_dynamic-update-slice_fusion), channel_id=1, source_target_pairs={{4,0},{8,4},{12,8},{0,12},{5,1},{9,5},{13,9},{1,13},{6,2},{10,6},{... | collective-permute-start | bytes 110600 | tf_op jit(solution)/shard_map/ppermute | solution.py:34
  26.9 5.9 %collective-permute-start.4 = (f32[3,1,1,4,768]{4,3,2,1,0:T(4,128)S(1)}, f32[3,1,1,4,768]{4,3,2,1,0:T(4,128)S(1)}, u32[]{:S(2)}, u32[]{:S(2)}) collective-permute-start(f32[3,1,1,4,768]{4,3,2,1,0:T(4,128)S(1)} %constant_dynamic-update-slice_fusion), channel_id=1, source_target_pairs={{0,4},{4,8},{8,12},{12,0},{1,5},{5,9},{9,13},{13,1},{2,6},{6,10},{... | collective-permute-start | bytes 110600 | tf_op jit(solution)/shard_map/ppermute | solution.py:33
  32.9 7.2 %collective-permute-start.7 = (f32[3,3,1,4,768]{4,3,2,1,0:T(4,128)S(1)}, f32[3,3,1,4,768]{4,3,2,1,0:T(4,128)S(1)}, u32[]{:S(2)}, u32[]{:S(2)}) collective-permute-start(f32[3,3,1,4,768]{4,3,2,1,0:T(4,128)S(1)} %pad_maximum_fusion.1), channel_id=1, source_target_pairs={{1,0},{2,1},{3,2},{0,3},{5,4},{6,5},{7,6},{4,7},{9,8},{10,9},{11,1... | collective-permute-start | bytes 331784 | tf_op jit(solution)/shard_map/ppermute | solution.py:34
  37.8 7.9 %collective-permute-start.6 = (f32[3,3,1,4,768]{4,3,2,1,0:T(4,128)S(1)}, f32[3,3,1,4,768]{4,3,2,1,0:T(4,128)S(1)}, u32[]{:S(2)}, u32[]{:S(2)}) collective-permute-start(f32[3,3,1,4,768]{4,3,2,1,0:T(4,128)S(1)} %pad_maximum_fusion.1), channel_id=1, source_target_pairs={{0,1},{1,2},{2,3},{3,0},{4,5},{5,6},{6,7},{7,4},{8,9},{9,10},{10,1... | collective-permute-start | bytes 331784 | tf_op jit(solution)/shard_map/ppermute | solution.py:33
  151.1 5.2 %collective-permute-start.16 = (f32[3,768]{1,0:T(4,128)S(1)}, f32[3,768]{1,0:T(4,128)S(1)}, u32[]{:S(2)}, u32[]{:S(2)}) collective-permute-start(f32[3,768]{1,0:T(4,128)S(1)} %get-tuple-element.40), channel_id=1, source_target_pairs={{0,496},{16,0},{32,16},{48,32},{64,48},{80,64},{96,80},{112,96},{1... | collective-permute-start | bytes 27656 | tf_op jit(solution)/shard_map/ppermute | solution.py:23
  159.3 6.8 %collective-permute-start.49 = (f32[3,768]{1,0:T(4,128)S(1)}, f32[3,768]{1,0:T(4,128)S(1)}, u32[]{:S(2)}, u32[]{:S(2)}) collective-permute-start(f32[3,768]{1,0:T(4,128)S(1)} %get-tuple-element.22), channel_id=1, source_target_pairs={{0,16},{16,32},{32,48},{48,64},{64,80},{80,96},{96,112},{112,128},... | collective-permute-start | bytes 27656 | tf_op jit(solution)/shard_map/ppermute | solution.py:23
  159.4 9.6 %collective-permute-start.46 = (f32[3,768]{1,0:T(4,128)S(1)}, f32[3,768]{1,0:T(4,128)S(1)}, u32[]{:S(2)}, u32[]{:S(2)}) collective-permute-start(f32[3,768]{1,0:T(4,128)S(1)} %get-tuple-element.23), channel_id=1, source_target_pairs={{0,16},{16,32},{32,48},{48,64},{64,80},{80,96},{96,112},{112,128},... | collective-permute-start | bytes 27656 | tf_op jit(solution)/shard_map/ppermute | solution.py:23
  160.6 10.4 %collective-permute-start.44 = (f32[3,768]{1,0:T(4,128)S(1)}, f32[3,768]{1,0:T(4,128)S(1)}, u32[]{:S(2)}, u32[]{:S(2)}) collective-permute-start(f32[3,768]{1,0:T(4,128)S(1)} %get-tuple-element.24), channel_id=1, source_target_pairs={{0,16},{16,32},{32,48},{48,64},{64,80},{80,96},{96,112},{112,128},... | collective-permute-start | bytes 27656 | tf_op jit(solution)/shard_map/ppermute | solution.py:23
  160.8 12.2 %collective-permute-start.41 = (f32[3,768]{1,0:T(4,128)S(1)}, f32[3,768]{1,0:T(4,128)S(1)}, u32[]{:S(2)}, u32[]{:S(2)}) collective-permute-start(f32[3,768]{1,0:T(4,128)S(1)} %get-tuple-element.25), channel_id=1, source_target_pairs={{0,16},{16,32},{32,48},{48,64},{64,80},{80,96},{96,112},{112,128},... | collective-permute-start | bytes 27656 | tf_op jit(solution)/shard_map/ppermute | solution.py:23
  160.9 17.2 %collective-permute-start.39 = (f32[3,768]{1,0:T(4,128)S(1)}, f32[3,768]{1,0:T(4,128)S(1)}, u32[]{:S(2)}, u32[]{:S(2)}) collective-permute-start(f32[3,768]{1,0:T(4,128)S(1)} %get-tuple-element.26), channel_id=1, source_target_pairs={{0,4},{4,8},{8,12},{12,0},{1,5},{5,9},{9,13},{13,1},{2,6},{6,10},{... | collective-permute-start | bytes 27656 | tf_op jit(solution)/shard_map/ppermute | solution.py:23
  166.1 15.9 %collective-permute-start.38 = (f32[3,768]{1,0:T(4,128)S(1)}, f32[3,768]{1,0:T(4,128)S(1)}, u32[]{:S(2)}, u32[]{:S(2)}) collective-permute-start(f32[3,768]{1,0:T(4,128)S(1)} %get-tuple-element.27), channel_id=1, source_target_pairs={{0,4},{4,8},{8,12},{12,0},{1,5},{5,9},{9,13},{13,1},{2,6},{6,10},{... | collective-permute-start | bytes 27656 | tf_op jit(solution)/shard_map/ppermute | solution.py:23
  169.1 15.9 %collective-permute-start.36 = (f32[3,768]{1,0:T(4,128)S(1)}, f32[3,768]{1,0:T(4,128)S(1)}, u32[]{:S(2)}, u32[]{:S(2)}) collective-permute-start(f32[3,768]{1,0:T(4,128)S(1)} %get-tuple-element.28), channel_id=1, source_target_pairs={{0,4},{4,8},{8,12},{12,0},{1,5},{5,9},{9,13},{13,1},{2,6},{6,10},{... | collective-permute-start | bytes 27656 | tf_op jit(solution)/shard_map/ppermute | solution.py:23
  171.0 15.9 %collective-permute-start.35 = (f32[3,768]{1,0:T(4,128)S(1)}, f32[3,768]{1,0:T(4,128)S(1)}, u32[]{:S(2)}, u32[]{:S(2)}) collective-permute-start(f32[3,768]{1,0:T(4,128)S(1)} %get-tuple-element.29), channel_id=1, source_target_pairs={{0,1},{1,2},{2,3},{3,0},{4,5},{5,6},{6,7},{7,4},{8,9},{9,10},{10,1... | collective-permute-start | bytes 27656 | tf_op jit(solution)/shard_map/ppermute | solution.py:23
  173.0 14.4 %collective-permute-start.34 = (f32[3,768]{1,0:T(4,128)S(1)}, f32[3,768]{1,0:T(4,128)S(1)}, u32[]{:S(2)}, u32[]{:S(2)}) collective-permute-start(f32[3,768]{1,0:T(4,128)S(1)} %get-tuple-element.30), channel_id=1, source_target_pairs={{0,3},{1,0},{2,1},{3,2},{4,7},{5,4},{6,5},{7,6},{8,11},{9,8},{10,9... | collective-permute-start | bytes 27656 | tf_op jit(solution)/shard_map/ppermute | solution.py:23
  178.1 12.4 %collective-permute-start.32 = (f32[3,768]{1,0:T(4,128)S(1)}, f32[3,768]{1,0:T(4,128)S(1)}, u32[]{:S(2)}, u32[]{:S(2)}) collective-permute-start(f32[3,768]{1,0:T(4,128)S(1)} %get-tuple-element.31), channel_id=1, source_target_pairs={{0,12},{4,0},{8,4},{12,8},{1,13},{5,1},{9,5},{13,9},{2,14},{6,2},{... | collective-permute-start | bytes 27656 | tf_op jit(solution)/shard_map/ppermute | solution.py:23
  182.0 12.4 %collective-permute-start.31 = (f32[3,768]{1,0:T(4,128)S(1)}, f32[3,768]{1,0:T(4,128)S(1)}, u32[]{:S(2)}, u32[]{:S(2)}) collective-permute-start(f32[3,768]{1,0:T(4,128)S(1)} %get-tuple-element.32), channel_id=1, source_target_pairs={{0,12},{4,0},{8,4},{12,8},{1,13},{5,1},{9,5},{13,9},{2,14},{6,2},{... | collective-permute-start | bytes 27656 | tf_op jit(solution)/shard_map/ppermute | solution.py:23
  185.0 13.1 %collective-permute-start.29 = (f32[3,768]{1,0:T(4,128)S(1)}, f32[3,768]{1,0:T(4,128)S(1)}, u32[]{:S(2)}, u32[]{:S(2)}) collective-permute-start(f32[3,768]{1,0:T(4,128)S(1)} %get-tuple-element.33), channel_id=1, source_target_pairs={{0,12},{4,0},{8,4},{12,8},{1,13},{5,1},{9,5},{13,9},{2,14},{6,2},{... | collective-permute-start | bytes 27656 | tf_op jit(solution)/shard_map/ppermute | solution.py:23
  186.9 13.1 %collective-permute-start.26 = (f32[3,768]{1,0:T(4,128)S(1)}, f32[3,768]{1,0:T(4,128)S(1)}, u32[]{:S(2)}, u32[]{:S(2)}) collective-permute-start(f32[3,768]{1,0:T(4,128)S(1)} %get-tuple-element.34), channel_id=1, source_target_pairs={{0,496},{16,0},{32,16},{48,32},{64,48},{80,64},{96,80},{112,96},{1... | collective-permute-start | bytes 27656 | tf_op jit(solution)/shard_map/ppermute | solution.py:23
  187.4 17.8 %collective-permute-start.12 = (f32[3,768]{1,0:T(4,128)S(1)}, f32[3,768]{1,0:T(4,128)S(1)}, u32[]{:S(2)}, u32[]{:S(2)}) collective-permute-start(f32[3,768]{1,0:T(4,128)S(1)} %collective-permute-done.11), channel_id=1, source_target_pairs={{0,12},{4,0},{8,4},{12,8},{1,13},{5,1},{9,5},{13,9},{2,14},{6,2},{... | collective-permute-start | bytes 27656 | tf_op jit(solution)/shard_map/ppermute | solution.py:23
  190.5 16.9 %collective-permute-start.25 = (f32[3,768]{1,0:T(4,128)S(1)}, f32[3,768]{1,0:T(4,128)S(1)}, u32[]{:S(2)}, u32[]{:S(2)}) collective-permute-start(f32[3,768]{1,0:T(4,128)S(1)} %collective-permute-done.24), channel_id=1, source_target_pairs={{0,4},{4,8},{8,12},{12,0},{1,5},{5,9},{9,13},{13,1},{2,6},{6,10},{... | collective-permute-start | bytes 27656 | tf_op jit(solution)/shard_map/ppermute | solution.py:23
  194.5 14.9 %collective-permute-start.22 = (f32[3,768]{1,0:T(4,128)S(1)}, f32[3,768]{1,0:T(4,128)S(1)}, u32[]{:S(2)}, u32[]{:S(2)}) collective-permute-start(f32[3,768]{1,0:T(4,128)S(1)} %collective-permute-done.21), channel_id=1, source_target_pairs={{0,4},{4,8},{8,12},{12,0},{1,5},{5,9},{9,13},{13,1},{2,6},{6,10},{... | collective-permute-start | bytes 27656 | tf_op jit(solution)/shard_map/ppermute | solution.py:23
  198.1 16.4 %collective-permute-start.20 = (f32[3,768]{1,0:T(4,128)S(1)}, f32[3,768]{1,0:T(4,128)S(1)}, u32[]{:S(2)}, u32[]{:S(2)}) collective-permute-start(f32[3,768]{1,0:T(4,128)S(1)} %collective-permute-done.19), channel_id=1, source_target_pairs={{0,1},{1,2},{2,3},{3,0},{4,5},{5,6},{6,7},{7,4},{8,9},{9,10},{10,1... | collective-permute-start | bytes 27656 | tf_op jit(solution)/shard_map/ppermute | solution.py:23
  200.1 18.1 %collective-permute-start.17 = (f32[3,768]{1,0:T(4,128)S(1)}, f32[3,768]{1,0:T(4,128)S(1)}, u32[]{:S(2)}, u32[]{:S(2)}) collective-permute-start(f32[3,768]{1,0:T(4,128)S(1)} %collective-permute-done.16), channel_id=1, source_target_pairs={{0,3},{1,0},{2,1},{3,2},{4,7},{5,4},{6,5},{7,6},{8,11},{9,8},{10,9... | collective-permute-start | bytes 27656 | tf_op jit(solution)/shard_map/ppermute | solution.py:23
  205.2 14.9 %collective-permute-start.14 = (f32[3,768]{1,0:T(4,128)S(1)}, f32[3,768]{1,0:T(4,128)S(1)}, u32[]{:S(2)}, u32[]{:S(2)}) collective-permute-start(f32[3,768]{1,0:T(4,128)S(1)} %collective-permute-done.13), channel_id=1, source_target_pairs={{0,12},{4,0},{8,4},{12,8},{1,13},{5,1},{9,5},{13,9},{2,14},{6,2},{... | collective-permute-start | bytes 27656 | tf_op jit(solution)/shard_map/ppermute | solution.py:23
  207.4 14.6 %collective-permute-start.9 = (f32[3,768]{1,0:T(4,128)S(1)}, f32[3,768]{1,0:T(4,128)S(1)}, u32[]{:S(2)}, u32[]{:S(2)}) collective-permute-start(f32[3,768]{1,0:T(4,128)S(1)} %collective-permute-done.8), channel_id=1, source_target_pairs={{0,12},{4,0},{8,4},{12,8},{1,13},{5,1},{9,5},{13,9},{2,14},{6,2},{... | collective-permute-start | bytes 27656 | tf_op jit(solution)/shard_map/ppermute | solution.py:23
  209.4 17.8 %collective-permute-start.60 = (f32[3,768]{1,0:T(4,128)S(1)}, f32[3,768]{1,0:T(4,128)S(1)}, u32[]{:S(2)}, u32[]{:S(2)}) collective-permute-start(f32[3,768]{1,0:T(4,128)S(1)} %collective-permute-done.59), channel_id=1, source_target_pairs={{0,4},{4,8},{8,12},{12,0},{1,5},{5,9},{9,13},{13,1},{2,6},{6,10},{... | collective-permute-start | bytes 27656 | tf_op jit(solution)/shard_map/ppermute | solution.py:23
  214.5 16.6 %collective-permute-start.58 = (f32[3,768]{1,0:T(4,128)S(1)}, f32[3,768]{1,0:T(4,128)S(1)}, u32[]{:S(2)}, u32[]{:S(2)}) collective-permute-start(f32[3,768]{1,0:T(4,128)S(1)} %collective-permute-done.57), channel_id=1, source_target_pairs={{0,4},{4,8},{8,12},{12,0},{1,5},{5,9},{9,13},{13,1},{2,6},{6,10},{... | collective-permute-start | bytes 27656 | tf_op jit(solution)/shard_map/ppermute | solution.py:23
  218.2 15.2 %collective-permute-start.55 = (f32[3,768]{1,0:T(4,128)S(1)}, f32[3,768]{1,0:T(4,128)S(1)}, u32[]{:S(2)}, u32[]{:S(2)}) collective-permute-start(f32[3,768]{1,0:T(4,128)S(1)} %collective-permute-done.54), channel_id=1, source_target_pairs={{0,4},{4,8},{8,12},{12,0},{1,5},{5,9},{9,13},{13,1},{2,6},{6,10},{... | collective-permute-start | bytes 27656 | tf_op jit(solution)/shard_map/ppermute | solution.py:23
  220.1 15.2 %collective-permute-start.53 = (f32[3,768]{1,0:T(4,128)S(1)}, f32[3,768]{1,0:T(4,128)S(1)}, u32[]{:S(2)}, u32[]{:S(2)}) collective-permute-start(f32[3,768]{1,0:T(4,128)S(1)} %collective-permute-done.52), channel_id=1, source_target_pairs={{0,1},{1,2},{2,3},{3,0},{4,5},{5,6},{6,7},{7,4},{8,9},{9,10},{10,1... | collective-permute-start | bytes 27656 | tf_op jit(solution)/shard_map/ppermute | solution.py:23
  222.1 15.2 %collective-permute-start.50 = (f32[3,768]{1,0:T(4,128)S(1)}, f32[3,768]{1,0:T(4,128)S(1)}, u32[]{:S(2)}, u32[]{:S(2)}) collective-permute-start(f32[3,768]{1,0:T(4,128)S(1)} %collective-permute-done.49), channel_id=1, source_target_pairs={{0,3},{1,0},{2,1},{3,2},{4,7},{5,4},{6,5},{7,6},{8,11},{9,8},{10,9... | collective-permute-start | bytes 27656 | tf_op jit(solution)/shard_map/ppermute | solution.py:23
  227.2 15.2 %collective-permute-start.47 = (f32[3,768]{1,0:T(4,128)S(1)}, f32[3,768]{1,0:T(4,128)S(1)}, u32[]{:S(2)}, u32[]{:S(2)}) collective-permute-start(f32[3,768]{1,0:T(4,128)S(1)} %collective-permute-done.46), channel_id=1, source_target_pairs={{0,12},{4,0},{8,4},{12,8},{1,13},{5,1},{9,5},{13,9},{2,14},{6,2},{... | collective-permute-start | bytes 27656 | tf_op jit(solution)/shard_map/ppermute | solution.py:23
  231.2 13.2 %collective-permute-start.45 = (f32[3,768]{1,0:T(4,128)S(1)}, f32[3,768]{1,0:T(4,128)S(1)}, u32[]{:S(2)}, u32[]{:S(2)}) collective-permute-start(f32[3,768]{1,0:T(4,128)S(1)} %collective-permute-done.44), channel_id=1, source_target_pairs={{0,12},{4,0},{8,4},{12,8},{1,13},{5,1},{9,5},{13,9},{2,14},{6,2},{... | collective-permute-start | bytes 27656 | tf_op jit(solution)/shard_map/ppermute | solution.py:23
  233.4 16.1 %collective-permute-start.42 = (f32[3,768]{1,0:T(4,128)S(1)}, f32[3,768]{1,0:T(4,128)S(1)}, u32[]{:S(2)}, u32[]{:S(2)}) collective-permute-start(f32[3,768]{1,0:T(4,128)S(1)} %collective-permute-done.41), channel_id=1, source_target_pairs={{0,12},{4,0},{8,4},{12,8},{1,13},{5,1},{9,5},{13,9},{2,14},{6,2},{... | collective-permute-start | bytes 27656 | tf_op jit(solution)/shard_map/ppermute | solution.py:23
  235.3 19.3 %collective-permute-start.40 = (f32[3,768]{1,0:T(4,128)S(1)}, f32[3,768]{1,0:T(4,128)S(1)}, u32[]{:S(2)}, u32[]{:S(2)}) collective-permute-start(f32[3,768]{1,0:T(4,128)S(1)} %collective-permute-done.39), channel_id=1, source_target_pairs={{0,1},{1,2},{2,3},{3,0},{4,5},{5,6},{6,7},{7,4},{8,9},{9,10},{10,1... | collective-permute-start | bytes 27656 | tf_op jit(solution)/shard_map/ppermute | solution.py:23
  237.3 19.3 %collective-permute-start.37 = (f32[3,768]{1,0:T(4,128)S(1)}, f32[3,768]{1,0:T(4,128)S(1)}, u32[]{:S(2)}, u32[]{:S(2)}) collective-permute-start(f32[3,768]{1,0:T(4,128)S(1)} %collective-permute-done.36), channel_id=1, source_target_pairs={{0,3},{1,0},{2,1},{3,2},{4,7},{5,4},{6,5},{7,6},{8,11},{9,8},{10,9... | collective-permute-start | bytes 27656 | tf_op jit(solution)/shard_map/ppermute | solution.py:23
  242.4 18.1 %collective-permute-start.33 = (f32[3,768]{1,0:T(4,128)S(1)}, f32[3,768]{1,0:T(4,128)S(1)}, u32[]{:S(2)}, u32[]{:S(2)}) collective-permute-start(f32[3,768]{1,0:T(4,128)S(1)} %collective-permute-done.32), channel_id=1, source_target_pairs={{0,1},{1,2},{2,3},{3,0},{4,5},{5,6},{6,7},{7,4},{8,9},{9,10},{10,1... | collective-permute-start | bytes 27656 | tf_op jit(solution)/shard_map/ppermute | solution.py:23
  244.4 19.9 %collective-permute-start.30 = (f32[3,768]{1,0:T(4,128)S(1)}, f32[3,768]{1,0:T(4,128)S(1)}, u32[]{:S(2)}, u32[]{:S(2)}) collective-permute-start(f32[3,768]{1,0:T(4,128)S(1)} %collective-permute-done.29), channel_id=1, source_target_pairs={{0,3},{1,0},{2,1},{3,2},{4,7},{5,4},{6,5},{7,6},{8,11},{9,8},{10,9... | collective-permute-start | bytes 27656 | tf_op jit(solution)/shard_map/ppermute | solution.py:23
  249.5 17.5 %collective-permute-start.27 = (f32[3,768]{1,0:T(4,128)S(1)}, f32[3,768]{1,0:T(4,128)S(1)}, u32[]{:S(2)}, u32[]{:S(2)}) collective-permute-start(f32[3,768]{1,0:T(4,128)S(1)} %collective-permute-done.26), channel_id=1, source_target_pairs={{0,4},{4,8},{8,12},{12,0},{1,5},{5,9},{9,13},{13,1},{2,6},{6,10},{... | collective-permute-start | bytes 27656 | tf_op jit(solution)/shard_map/ppermute | solution.py:23
  254.7 16.7 %collective-permute-start.23 = (f32[3,768]{1,0:T(4,128)S(1)}, f32[3,768]{1,0:T(4,128)S(1)}, u32[]{:S(2)}, u32[]{:S(2)}) collective-permute-start(f32[3,768]{1,0:T(4,128)S(1)} %collective-permute-done.22), channel_id=1, source_target_pairs={{0,3},{1,0},{2,1},{3,2},{4,7},{5,4},{6,5},{7,6},{8,11},{9,8},{10,9... | collective-permute-start | bytes 27656 | tf_op jit(solution)/shard_map/ppermute | solution.py:23
  256.6 16.7 %collective-permute-start.15 = (f32[3,768]{1,0:T(4,128)S(1)}, f32[3,768]{1,0:T(4,128)S(1)}, u32[]{:S(2)}, u32[]{:S(2)}) collective-permute-start(f32[3,768]{1,0:T(4,128)S(1)} %collective-permute-done.14), channel_id=1, source_target_pairs={{0,1},{1,2},{2,3},{3,0},{4,5},{5,6},{6,7},{7,4},{8,9},{9,10},{10,1... | collective-permute-start | bytes 27656 | tf_op jit(solution)/shard_map/ppermute | solution.py:23
  260.5 17.9 %collective-permute-start.10 = (f32[3,768]{1,0:T(4,128)S(1)}, f32[3,768]{1,0:T(4,128)S(1)}, u32[]{:S(2)}, u32[]{:S(2)}) collective-permute-start(f32[3,768]{1,0:T(4,128)S(1)} %collective-permute-done.9), channel_id=1, source_target_pairs={{0,3},{1,0},{2,1},{3,2},{4,7},{5,4},{6,5},{7,6},{8,11},{9,8},{10,9... | collective-permute-start | bytes 27656 | tf_op jit(solution)/shard_map/ppermute | solution.py:23
  264.3 16.7 %collective-permute-start.61 = (f32[3,768]{1,0:T(4,128)S(1)}, f32[3,768]{1,0:T(4,128)S(1)}, u32[]{:S(2)}, u32[]{:S(2)}) collective-permute-start(f32[3,768]{1,0:T(4,128)S(1)} %collective-permute-done.60), channel_id=1, source_target_pairs={{0,1},{1,2},{2,3},{3,0},{4,5},{5,6},{6,7},{7,4},{8,9},{9,10},{10,1... | collective-permute-start | bytes 27656 | tf_op jit(solution)/shard_map/ppermute | solution.py:23
  267.0 14.0 %collective-permute-start.56 = (f32[3,768]{1,0:T(4,128)S(1)}, f32[3,768]{1,0:T(4,128)S(1)}, u32[]{:S(2)}, u32[]{:S(2)}) collective-permute-start(f32[3,768]{1,0:T(4,128)S(1)} %collective-permute-done.55), channel_id=1, source_target_pairs={{0,3},{1,0},{2,1},{3,2},{4,7},{5,4},{6,5},{7,6},{8,11},{9,8},{10,9... | collective-permute-start | bytes 27656 | tf_op jit(solution)/shard_map/ppermute | solution.py:23
  271.3 9.6 %collective-permute-start.48 = (f32[3,768]{1,0:T(4,128)S(1)}, f32[3,768]{1,0:T(4,128)S(1)}, u32[]{:S(2)}, u32[]{:S(2)}) collective-permute-start(f32[3,768]{1,0:T(4,128)S(1)} %collective-permute-done.47), channel_id=1, source_target_pairs={{0,1},{1,2},{2,3},{3,0},{4,5},{5,6},{6,7},{7,4},{8,9},{9,10},{10,1... | collective-permute-start | bytes 27656 | tf_op jit(solution)/shard_map/ppermute | solution.py:23
  273.3 7.7 %collective-permute-start.43 = (f32[3,768]{1,0:T(4,128)S(1)}, f32[3,768]{1,0:T(4,128)S(1)}, u32[]{:S(2)}, u32[]{:S(2)}) collective-permute-start(f32[3,768]{1,0:T(4,128)S(1)} %collective-permute-done.42), channel_id=1, source_target_pairs={{0,3},{1,0},{2,1},{3,2},{4,7},{5,4},{6,5},{7,6},{8,11},{9,8},{10,9... | collective-permute-start | bytes 27656 | tf_op jit(solution)/shard_map/ppermute | solution.py:23
  278.4 6.8 %collective-permute-start.28 = (f32[3,768]{1,0:T(4,128)S(1)}, f32[3,768]{1,0:T(4,128)S(1)}, u32[]{:S(2)}, u32[]{:S(2)}) collective-permute-start(f32[3,768]{1,0:T(4,128)S(1)} %collective-permute-done.27), channel_id=1, source_target_pairs={{0,1},{1,2},{2,3},{3,0},{4,5},{5,6},{6,7},{7,4},{8,9},{9,10},{10,1... | collective-permute-start | bytes 27656 | tf_op jit(solution)/shard_map/ppermute | solution.py:23
  (36 other events, 975.1 us)
where the time goes:
time: 288 us; the launch traced here: 286 us
  starting transfers between devices  153 us (53%)
  other arithmetic  59.7 us (21%)
  local copies, waits for them, and re-layouts  38.6 us (13%)
  waiting for transfers between devices  15.7 us (5%)
  matrix products  14.9 us (5%)
  between operations  3.88 us (1%)
    ppermute x56, starting transfers between devices, passed_along(): return lax.ppermute(value, axis, pairs)  136 us
    add_any x1, other arithmetic, pair_energy(): displacement = flat_pos[:, neighbour] - flat_pos[:, centre_ext]  10.9 us
    ppermute x3, starting transfers between devices, with_halo(): after = lax.ppermute(first, axis, down)  10.6 us
    gather x4, local copies, waits for them, and re-layouts, pair_energy(): displacement = flat_pos[:, neighbour] - flat_pos[:, centre_ext]  10.4 us
    add x1, other arithmetic, on_device(): ext_pos = extended[:, :3] + edge_length * offset_table()[:, :, None]  9.37 us
    neg x1, other arithmetic, on_device(): partial_value = -pullback(jnp.ones((), jnp.float32))[0]  9.05 us
    ppermute x56, waiting for transfers between devices, passed_along(): return lax.ppermute(value, axis, pairs)  8.13 us
    scatter-add x2, other arithmetic, pair_energy(): centre_env = environment[:, centre].reshape(4, MULT, pair_total)  7.47 us
  transfers between devices with their start and end apart: 62, of which 11 were waited for; matrix products, arithmetic and copies ran while one was open for 2% of the time, Pallas kernels for 0%

commit v1 on v0

v1 whole, which is shorter than its diff:
```python
import functools

import jax
import jax.numpy as jnp
from jax import lax
from jax.experimental import pallas as pl
from jax.experimental.pallas import tpu as pltpu
from jax.sharding import PartitionSpec as P

MESH = pl.DeviceIdType.MESH

CH = 256
MULT = 64
NBASIS = 8
NSPEC = 3
BLK = 128
NB = 4
PAIRS = 512
CHUNK = 256
CHUNKS = PAIRS // CHUNK

EDGE = 1.5
CUTOFF = 9.0
SOFT2 = 0.25

GROUP = 18
FIRST = {-2: 0, -1: 1, 0: 6, 1: 12, 2: 17}
SENT = {-2: (5, 1), -1: (1, 5), 0: (0, 6), 1: (0, 5), 2: (0, 1)}
ROWS = 9 * GROUP
PADDED = 176
OWN = 4 * GROUP + FIRST[0]

F32 = jnp.float32
BF16 = jnp.bfloat16


def dot(a, b):
    return lax.dot_general(a, b, (((1,), (0,)), ((), ())), preferred_element_type=F32)


def dot_tn(a, b):
    return lax.dot_general(a, b, (((0,), (0,)), ((), ())), preferred_element_type=F32)


def dot_nt(a, b):
    return lax.dot_general(a, b, (((1,), (1,)), ((), ())), preferred_element_type=F32)


def halves(x):
    high = x.astype(BF16)
    return high, (x - high.astype(F32)).astype(BF16)


def rows_of(shape):
    return lax.broadcasted_iota(jnp.int32, shape, 0)


def series(u, terms):
    total = jnp.full_like(u, terms[-1])
    for term in terms[-2::-1]:
        total = total * u + term
    return total


def sin_cos_half_turns(t):
    k = jnp.floor(t + 0.5)
    f = (t - k) * 3.14159265358979
    sign = 1.0 - 2.0 * (k - 2.0 * jnp.floor(0.5 * k))
    u = f * f
    sine = f * series(u, [1.0, -1 / 6, 1 / 120, -1 / 5040, 1 / 362880, -1 / 39916800, 1 / 6227020800])
    cosine = series(
        u, [1.0, -1 / 2, 1 / 24, -1 / 720, 1 / 40320, -1 / 3628800, 1 / 479001600, -1 / 87178291200]
    )
    return sign * sine, sign * cosine


def silu_parts(x):
    gate = 0.5 + 0.5 * jnp.tanh(0.5 * x)
    value = x * gate
    return value, gate + value * (1.0 - gate)


def kernel(
    sizes,
    pos_hbm, kind_hbm, plan_hbm, centre_hbm, neighbour_hbm, blocks_hbm,
    w_in_hbm, w_hidden_hbm, w_env_hbm, w_latent_hbm, w_out_hbm,
    forces_ref, energy_ref,
    pos, kind, plan, centre, neighbour, blocks,
    w_in_raw, w_hidden, w_env, w_latent_t, w_out,
    w_in_t, w_in, w_hidden_t, w_back, w_latent,
    mine, held, lane_neighbour, lane_centre, same,
    d1, d2, h2, latent, grad, inners, dz, env_w, env_a, stacked_a, stacked_b,
    partial, arrived,
    in_sems, send_sem, recv_sem, back_send_sem, back_recv_sem,
):
    place = [lax.axis_index(axis) for axis in ("gx", "gy", "gz")]

    def device(steps):
        return tuple(
            lax.rem(at + (step + size), size) if step else at
            for at, step, size in zip(place, steps, sizes)
        )

    far = [(a, b, c) for b in (-1, 0, 1) for c in (-1, 0, 1) for a in (-2, -1, 0, 1, 2)]
    far = [o for o in far if o != (0, 0, 0)]
    far.sort(key=lambda o: -(abs(o[0]) + abs(o[1]) + abs(o[2])))
    near = [o for o in far if abs(o[0]) < 2]

    pairs_in = [
        (pos_hbm.at[0, 0], pos),
        (kind_hbm.at[0, 0], kind),
        (plan_hbm.at[0, 0], plan),
        (centre_hbm.at[0, 0], centre),
        (neighbour_hbm.at[0, 0], neighbour),
        (blocks_hbm.at[0], blocks),
        (w_in_hbm, w_in_raw),
        (w_hidden_hbm, w_hidden),
        (w_env_hbm, w_env),
        (w_latent_hbm, w_latent_t),
        (w_out_hbm, w_out),
    ]
    loads = [
        pltpu.make_async_copy(source, target, in_sems.at[i])
        for i, (source, target) in enumerate(pairs_in)
    ]
    for load in loads:
        load.start()

    barrier = pltpu.get_barrier_semaphore()
    for offset in far:
        pl.semaphore_signal(barrier, inc=1, device_id=device(offset), device_id_type=MESH)

    for load in loads[:3]:
        load.wait()
    kind_rows = kind[...].astype(F32) + 1.0
    for b in range(NB):
        lanes_of = slice(b * BLK, (b + 1) * BLK)
        for c in range(3):
            mine[1 + b, c : c + 1] = pos[c, :, lanes_of]
        mine[1 + b, 3:4] = kind_rows[:, lanes_of]
    first_row = (rows_of((4, BLK)) == 0).astype(F32)
    for slot, move, shift in ((0, 1, -EDGE), (5, 2, EDGE)):
        packed = jnp.zeros((4, BLK), F32)
        for b in range(NB):
            chosen = jnp.where(plan[0, b] == move, 1.0, 0.0).astype(F32)
            packed = packed + chosen * (mine[1 + b] + shift * first_row)
        mine[slot] = packed
    held[OWN : OWN + 6] = mine[...]

    pl.semaphore_wait(barrier, len(far))
    for offset in far:
        a, b, c = offset
        start, count = SENT[a]
        where = (3 * (1 - b) + (1 - c)) * GROUP + FIRST[-a]
        pltpu.make_async_remote_copy(
            src_ref=mine.at[pl.ds(start, count)],
            dst_ref=held.at[pl.ds(where, count)],
            send_sem=send_sem,
            recv_sem=recv_sem,
            device_id=device(offset),
            device_id_type=MESH,
        ).start()

    for load in loads[3:]:
        load.wait()
    centre_row = centre[...]
    neighbour_row = neighbour[...]
    live = jnp.where(
        lax.broadcasted_iota(jnp.int32, (1, PAIRS), 1) < blocks[0, 0] * BLK, 1.0, 0.0
    ).astype(F32)
    centre_block = centre_row >> 7
    centre_lane = centre_row & 127
    block = neighbour_row >> 7
    neighbour_lane = neighbour_row & 127
    box = (block * 10923) >> 16
    k = block - 6 * box
    box_x = (box * 7282) >> 16
    box_yz = box - 9 * box_x
    box_y = (box_yz * 21846) >> 16
    box_z = box_yz - 3 * box_y

    def held_row(x, yz, k):
        up = jnp.where(x == 2, 6, x)
        down = jnp.where(x == 0, 11, 15 + x)
        return yz * GROUP + jnp.where(k == 0, up, jnp.where(k == 5, down, 1 + 5 * x + k))

    neighbour_held = held_row(box_x, box_yz, k)
    centre_held = held_row(jnp.ones_like(centre_block), jnp.zeros_like(centre_block), centre_block)
    lanes = rows_of((BLK, PAIRS))
    hot = jnp.where(lanes == neighbour_lane, 1.0, 0.0).astype(BF16)
    lane_neighbour[:BLK] = hot
    lane_neighbour[BLK:] = hot
    hot = jnp.where(lanes == centre_lane, 1.0, 0.0).astype(BF16)
    lane_centre[:BLK] = hot
    lane_centre[BLK:] = hot
    centre_column = jnp.transpose(
        jnp.broadcast_to(centre_row.astype(F32), (8, PAIRS)), (1, 0)
    )[:, 0:1]
    same[...] = jnp.where(centre_column == centre_row.astype(F32), 1.0, 0.0).astype(F32)

    w_hidden_t[...] = jnp.transpose(w_hidden[...].astype(F32), (1, 0)).astype(BF16)
    for l in range(2):
        padding = jnp.zeros((BLK - MULT, CH), F32)
        rows = jnp.concatenate([w_env[l].astype(F32), padding], axis=0)
        w_back[l, :, :CH] = w_latent_t[l, :CH]
        w_back[l, :, CH:] = jnp.transpose(rows, (1, 0)).astype(BF16)
        rows = jnp.concatenate([w_latent_t[l].astype(F32), padding], axis=0)
        w_latent[l] = jnp.transpose(rows, (1, 0)).astype(BF16)
    fewer = NBASIS + 2 * NSPEC
    rows = jnp.concatenate([w_in_raw[...].astype(F32), jnp.zeros((BLK - fewer, CH), F32)], axis=0)
    w_in_t[...] = rows[:16].astype(BF16)
    w_in[...] = jnp.transpose(rows, (1, 0)).astype(BF16)
    no_rows = jnp.zeros((BLK - MULT, CHUNK), BF16)
    out_row = jnp.concatenate([w_out[0:1], w_out[1:2]], axis=1)
    out_column = jnp.transpose(jnp.broadcast_to(out_row.astype(F32), (8, CH)), (1, 0))[:, 0:1]
    grad[...] = out_column * live

    incoming = ROWS - 6
    pltpu.make_async_copy(
        held.at[pl.ds(0, incoming)], held.at[pl.ds(0, incoming)], recv_sem
    ).wait()

    neighbour_mask = rows_of((ROWS, PAIRS)) == neighbour_held
    centre_mask = rows_of((GROUP, PAIRS)) == centre_held
    near_rows = []
    own_rows = []
    for c in range(4):
        table = held[:, c, :]
        high, low = halves(table)
        both = jnp.concatenate([high, low], axis=1)
        found = dot(both, lane_neighbour[...])
        near_rows.append(jnp.sum(jnp.where(neighbour_mask, found, 0.0), axis=0, keepdims=True))
        table = held[4 * GROUP : 5 * GROUP, c, :]
        high, low = halves(table)
        both = jnp.concatenate([high, low], axis=1)
        found = dot(both, lane_centre[...])
        own_rows.append(jnp.sum(jnp.where(centre_mask, found, 0.0), axis=0, keepdims=True))

    shifts = [EDGE * (v.astype(F32) - 1.0) for v in (box_x, box_y, box_z)]
    gap = [near_rows[c] + shifts[c] - own_rows[c] for c in range(3)]
    square = gap[0] * gap[0] + gap[1] * gap[1] + gap[2] * gap[2]
    inverse = lax.rsqrt(square + SOFT2)
    distance = (square + SOFT2) * inverse
    way = [g * inverse for g in gap]
    scaled = distance * (1.0 / CUTOFF)
    falling = 1.0 - scaled * scaled
    envelope = falling * falling
    orders = (rows_of((NBASIS, PAIRS)) + 1).astype(F32)
    sine, cosine = sin_cos_half_turns(orders * scaled)
    over = sine * inverse
    radial = over * envelope
    r8 = rows_of((8, PAIRS)).astype(F32)
    own_kind = own_rows[3] - 1.0
    near_kind = near_rows[3] - 1.0
    one_hots = jnp.where(
        r8 < NSPEC,
        jnp.where(r8 == own_kind, 1.0, 0.0),
        jnp.where(r8 - NSPEC == near_kind, jnp.where(r8 < 2 * NSPEC, 1.0, 0.0), 0.0),
    )
    features = jnp.concatenate(
        [radial, one_hots, jnp.zeros((BLK - 16, PAIRS), F32)], axis=0
    ).astype(BF16)

    y4 = jnp.concatenate([jnp.ones_like(distance)] + way, axis=0)
    y_high, y_low = halves(y4)
    none = jnp.zeros_like(y_high)
    products = dot_tn(
        jnp.concatenate([y_high, y_high, y_low, none], axis=0).astype(F32),
        jnp.concatenate([y_high, y_low, y_high, none], axis=0).astype(F32),
    )
    g_matrix = (same[...] * products).astype(BF16)

    spans = [slice(j * CHUNK, (j + 1) * CHUNK) for j in range(CHUNKS)]

    before = []
    for s in spans:
        value, slope = silu_parts(dot(w_in[...], features[:, s]))
        d1[:, s] = slope
        value, slope = silu_parts(dot(w_hidden[...], value.astype(BF16)))
        d2[:, s] = slope
        h2[:, s] = value
        latent[:, s] = value * envelope[:, s]
    for l in range(2):
        for j, s in enumerate(spans):
            half = latent[:, s].astype(BF16)
            env_w[l, :, s] = dot(w_env[l], half) * live[:, s]
            dz[l, :, s] = dot(w_latent[l, :, :CH], half)
        weights_half = env_w[l].astype(BF16)
        for j, s in enumerate(spans):
            gathered = dot(weights_half, g_matrix[:, s])
            env_a[l, :, s] = gathered
            invariant = (0.5 * env_w[l, :, s] * gathered).astype(BF16)
            value, slope = silu_parts(dz[l, :, s] + dot(w_latent[l, :, CH:], jnp.concatenate([invariant, no_rows], axis=0)))
            dz[l, :, s] = slope
            latent[:, s] = latent[:, s] + value
    energy = jnp.zeros((1, 1), F32)
    for s in spans:
        values = dot(out_row, latent[:, s].astype(BF16))
        energy = energy + jnp.sum(values * live[:, s], axis=1, keepdims=True)
    energy_ref[0] = energy

    for l in (1, 0):
        for s in spans:
            inner = (grad[:, s] * dz[l, :, s]).astype(BF16)
            inners[:, s] = inner
            d_invariant = 0.5 * dot(w_latent_t[l, CH:], inner)
            stacked_a[(2 + l) * MULT : (3 + l) * MULT, s] = d_invariant * env_w[l, :, s]
            env_a[l, :, s] = d_invariant * env_a[l, :, s]
        d_gathered = stacked_a[(2 + l) * MULT : (3 + l) * MULT, :].astype(BF16)
        for s in spans:
            d_weights = (env_a[l, :, s] + dot(d_gathered, g_matrix[:, s])) * live[:, s]
            both = jnp.concatenate([inners[:, s], d_weights.astype(BF16), no_rows], axis=0)
            grad[:, s] = grad[:, s] + dot(w_back[l], both)
    d_radial = []
    d_envelope = []
    for s in spans:
        d_latent = grad[:, s]
        d_envelope.append(jnp.sum(d_latent * h2[:, s], axis=0, keepdims=True))
        inner = (d_latent * envelope[:, s] * d2[:, s]).astype(BF16)
        inner = (dot(w_hidden_t[...], inner) * d1[:, s]).astype(BF16)
        d_radial.append(dot(w_in_t[...], inner)[:NBASIS])
    d_radial = jnp.concatenate(d_radial, axis=1)
    d_envelope = jnp.concatenate(d_envelope, axis=1)

    for l in range(2):
        stacked_a[l * MULT : (l + 1) * MULT, :] = env_w[l]
        stacked_b[l * MULT : (l + 1) * MULT, :] = stacked_a[(2 + l) * MULT : (3 + l) * MULT, :].astype(BF16)
        stacked_b[(2 + l) * MULT : (3 + l) * MULT, :] = env_w[l].astype(BF16)
    left = jnp.transpose(stacked_a[...], (1, 0)).astype(BF16)
    d_products = (same[...] * dot(left, stacked_b[...])).astype(BF16)
    d_y = dot(y_high, d_products)
    d_way = [d_y[1 + c : 2 + c] for c in range(3)]

    slope_envelope = falling * scaled * (-4.0 / CUTOFF)
    d_envelope = d_envelope + jnp.sum(d_radial * over, axis=0, keepdims=True)
    d_over = d_radial * envelope
    turning = cosine * orders * (3.14159265358979 / CUTOFF) - over
    d_distance = (
        d_envelope * slope_envelope
        + inverse * jnp.sum(d_over * turning, axis=0, keepdims=True)
        - inverse * (d_way[0] * way[0] + d_way[1] * way[1] + d_way[2] * way[2])
    )
    gradient = [d_way[c] * inverse + d_distance * way[c] for c in range(3)]

    g8 = jnp.concatenate(gradient + [jnp.zeros((5, PAIRS), F32)], axis=0)
    g_high = g8.astype(BF16).astype(F32)
    g_low = g8 - g_high
    block_mask = rows_of((PADDED, PAIRS)) == block
    for c in range(3):
        high, low = -g_high[c : c + 1], -g_low[c : c + 1]
        spread = jnp.concatenate(
            [
                jnp.where(block_mask, high, 0.0).astype(BF16),
                jnp.where(block_mask, low, 0.0).astype(BF16),
            ],
            axis=0,
        )
        both = dot_nt(spread, lane_neighbour[:BLK])
        partial[:, c, :] = both[:ROWS] + both[PADDED : PADDED + ROWS]
    for offset in near:
        a, b, c = offset
        at = 9 * (a + 1) + 3 * (b + 1) + (c + 1)
        pltpu.make_async_remote_copy(
            src_ref=partial.at[pl.ds(6 * at, 6)],
            dst_ref=arrived.at[pl.ds(6 * at, 6)],
            send_sem=back_send_sem,
            recv_sem=back_recv_sem,
            device_id=device(offset),
            device_id_type=MESH,
        ).start()
    arrived[6 * 13 : 6 * 14] = partial[6 * 13 : 6 * 14]
    own_mask = rows_of((8, PAIRS)) == centre_block
    own_parts = []
    for c in range(3):
        high, low = g_high[c : c + 1], g_low[c : c + 1]
        spread = jnp.concatenate(
            [
                jnp.where(own_mask, high, 0.0),
                jnp.where(own_mask, low, 0.0),
            ],
            axis=0,
        ).astype(BF16)
        both = dot_nt(spread, lane_centre[:BLK])
        own_parts.append(both[:8] + both[8:])
    pltpu.make_async_copy(
        arrived.at[pl.ds(0, 6 * 26)], arrived.at[pl.ds(0, 6 * 26)], back_recv_sem
    ).wait()
    for s in range(6):
        total = arrived[s]
        for o in range(1, 27):
            total = total + arrived[6 * o + s]
        for c in range(3):
            forces_ref[0, 0, c, :, s * BLK : (s + 1) * BLK] = (
                total[c : c + 1] + own_parts[c][s : s + 1]
            )

    pltpu.make_async_copy(
        held.at[pl.ds(0, incoming)], held.at[pl.ds(0, incoming)], send_sem
    ).wait()
    pltpu.make_async_copy(
        partial.at[pl.ds(0, 6 * 26)], partial.at[pl.ds(0, 6 * 26)], back_send_sem
    ).wait()


def on_device(sizes, positions, *arrays):
    *arrays, w_in, w_hidden, w_env, w_latent, w_out = arrays
    vmem = pltpu.VMEM
    forces, energy = pl.pallas_call(
        functools.partial(kernel, sizes),
        out_shape=(
            jax.ShapeDtypeStruct((1, 1, 3, 1, 6 * BLK), F32),
            jax.ShapeDtypeStruct((1, 1, 1), F32),
        ),
        in_specs=[pl.BlockSpec(memory_space=pltpu.HBM)] * 11,
        out_specs=(pl.BlockSpec(memory_space=vmem),) * 2,
        scratch_shapes=[
            vmem((3, 1, NB * BLK), F32),
            vmem((1, NB * BLK), jnp.int32),
            pltpu.SMEM((1, NB), jnp.int32),
            vmem((1, PAIRS), jnp.int32),
            vmem((1, PAIRS), jnp.int32),
            pltpu.SMEM((1, 1), jnp.int32),
            vmem((NBASIS + 2 * NSPEC, CH), BF16),
            vmem((CH, CH), BF16),
            vmem((2, MULT, CH), BF16),
            vmem((2, CH + MULT, CH), BF16),
            vmem((2, CH // 2), BF16),
            vmem((16, CH), BF16),
            vmem((CH, BLK), BF16),
            vmem((CH, CH), BF16),
            vmem((2, CH, CH + BLK), BF16),
            vmem((2, CH, CH + BLK), BF16),
            vmem((6, 4, BLK), F32),
            vmem((ROWS, 4, BLK), F32),
            vmem((2 * BLK, PAIRS), BF16),
            vmem((2 * BLK, PAIRS), BF16),
            vmem((PAIRS, PAIRS), F32),
            vmem((CH, PAIRS), F32),
            vmem((CH, PAIRS), F32),
            vmem((CH, PAIRS), F32),
            vmem((CH, PAIRS), F32),
            vmem((CH, PAIRS), F32),
            vmem((CH, PAIRS), BF16),
            vmem((2, CH, PAIRS), F32),
            vmem((2, MULT, PAIRS), F32),
            vmem((2, MULT, PAIRS), F32),
            vmem((4 * MULT, PAIRS), F32),
            vmem((4 * MULT, PAIRS), BF16),
            vmem((6 * 27, 4, BLK), F32),
            vmem((6 * 27, 4, BLK), F32),
            pltpu.SemaphoreType.DMA((11,)),
            pltpu.SemaphoreType.DMA,
            pltpu.SemaphoreType.DMA,
            pltpu.SemaphoreType.DMA,
            pltpu.SemaphoreType.DMA,
        ],
        compiler_params=pltpu.CompilerParams(
            collective_id=0, has_side_effects=True, vmem_limit_bytes=63 * 1024 * 1024
        ),
        cost_estimate=pl.CostEstimate(flops=10**9, bytes_accessed=10**6, transcendentals=10**6),
    )(
        positions.transpose(0, 1, 3, 2, 4),
        *arrays,
        w_in.T,
        w_hidden,
        w_env,
        w_latent.transpose(0, 2, 1),
        w_out.reshape(2, CH // 2),
    )
    return forces.transpose(0, 1, 3, 2, 4), energy


def solution(mesh):
    sizes = tuple(mesh.shape[axis] for axis in ("gx", "gy", "gz"))
    return jax.shard_map(
        functools.partial(on_device, sizes),
        mesh=mesh,
        in_specs=(
            P("gx", "gy", "gz", None, None),
            P("gx", "gy", "gz", None),
            P("gx", "gy", "gz", None),
            P("gx", "gy", "gz", None),
            P("gx", "gy", "gz", None),
            P("gx", "gy", "gz"),
            P(),
            P(),
            P(),
            P(),
            P(),
        ),
        out_specs=(P("gx", "gy", "gz", None, None), P("gx", "gy", "gz")),
        check_vma=False,
    )
```

time: 288 us -> 36.7 us (0.13)
  the two profiles are of different devices: /device:TPU:6 before, /device:TPU:1 now
where the time goes in v1:
time: 36.7 us; the launch traced here: 36.4 us
  Pallas kernels  32.1 us (87%)
  between operations  3.05 us (8%)
  local copies, waits for them, and re-layouts  1.3 us (4%)
    pallas_call x1, Pallas kernels, on_device(): pl.pallas_call(functools.partial(kernel, sizes), out_shape=(jax.ShapeDtyp...  32.1 us
    unnamed x1, local copies, waits for them, and re-layouts  1.3 us

profile of v1, /device:TPU:1, one launch (start us, length us, event | category | flops | bytes accessed | tf_op | source)
XLA Modules:
  0.0 36.4 jit_solution(10495497867578672990)
XLA Ops:
  1.3 32.1 %shard_map.122 = (f32[1,1,3,1,768]{4,3,2,1,0:T(1,128)}, f32[1,1,1]{2,1,0:T(1,128)}) custom-call(f32[1,1,3,1,512]{4,3,2,1,0:T(1,128)} %bitcast.10, s32[1,1,1,512]{3,2,1,0:T(1,128)} %kind_hbm.1, s32[1,1,1,4]{3,2,1,0:T(1,128)} %plan_hbm.1, s32[1,1,1,512]{3,2,1,0:T(1,128)} %centre_hbm.1, s32[1,1,1,512]{3,2,1,0:T(1,128)} %neighbour_hbm.1, ...), custom_call_target="tpu_custom_call" | custom-call | flops 1000000000 | bytes 1000000 | tf_op jit(solution)/shard_map/pallas_call | solution.py:408
  33.4 1.3 %copy.17 = f32[1,1,1,3,768]{4,2,3,1,0:T(1,128)} copy(f32[1,1,1,3,768]{4,2,3,1,0:T(1,128)} %bitcast.7) | data formatting | bytes 18432

commit v2 on v1

--- a/solution.py
+++ b/solution.py
@@ -89,7 +89,7 @@
     w_in_raw, w_hidden, w_env, w_latent_t, w_out,
     w_in_t, w_in, w_hidden_t, w_back, w_latent,
     mine, held, lane_neighbour, lane_centre, same,
-    d1, d2, h2, latent, grad, inners, dz, env_w, env_a, stacked_a, stacked_b,
+    d1, d2, h2, latent, grad, inners, dz, env_w, env_a, stacked_a, stacked_b, left,
     partial, arrived,
     in_sems, send_sem, recv_sem, back_send_sem, back_recv_sem,
 ):
@@ -112,7 +112,6 @@
         (plan_hbm.at[0, 0], plan),
         (centre_hbm.at[0, 0], centre),
         (neighbour_hbm.at[0, 0], neighbour),
-        (blocks_hbm.at[0], blocks),
         (w_in_hbm, w_in_raw),
         (w_hidden_hbm, w_hidden),
         (w_env_hbm, w_env),
@@ -166,7 +165,7 @@
     centre_row = centre[...]
     neighbour_row = neighbour[...]
     live = jnp.where(
-        lax.broadcasted_iota(jnp.int32, (1, PAIRS), 1) < blocks[0, 0] * BLK, 1.0, 0.0
+        lax.broadcasted_iota(jnp.int32, (1, PAIRS), 1) < blocks_hbm[0, 0, 0] * BLK, 1.0, 0.0
     ).astype(F32)
     centre_block = centre_row >> 7
     centre_lane = centre_row & 127
@@ -293,11 +292,10 @@
             value, slope = silu_parts(dz[l, :, s] + dot(w_latent[l, :, CH:], jnp.concatenate([invariant, no_rows], axis=0)))
             dz[l, :, s] = slope
             latent[:, s] = latent[:, s] + value
-    energy = jnp.zeros((1, 1), F32)
-    for s in spans:
-        values = dot(out_row, latent[:, s].astype(BF16))
-        energy = energy + jnp.sum(values * live[:, s], axis=1, keepdims=True)
-    energy_ref[0] = energy
+    for l in range(2):
+        stacked_a[l * MULT : (l + 1) * MULT, :] = env_w[l]
+        stacked_b[(2 + l) * MULT : (3 + l) * MULT, :] = env_w[l].astype(BF16)
+    left[:, : 2 * MULT] = jnp.transpose(stacked_a[: 2 * MULT], (1, 0)).astype(BF16)
 
     for l in (1, 0):
         for s in spans:
@@ -307,6 +305,12 @@
             stacked_a[(2 + l) * MULT : (3 + l) * MULT, s] = d_invariant * env_w[l, :, s]
             env_a[l, :, s] = d_invariant * env_a[l, :, s]
         d_gathered = stacked_a[(2 + l) * MULT : (3 + l) * MULT, :].astype(BF16)
+        stacked_b[l * MULT : (l + 1) * MULT, :] = d_gathered
+        if l == 0:
+            left[:, 2 * MULT :] = jnp.transpose(stacked_a[2 * MULT :], (1, 0)).astype(BF16)
+            d_products = (same[...] * dot(left[...], stacked_b[...])).astype(BF16)
+            d_y = dot(y_high, d_products)
+            d_way = [d_y[1 + c : 2 + c] for c in range(3)]
         for s in spans:
             d_weights = (env_a[l, :, s] + dot(d_gathered, g_matrix[:, s])) * live[:, s]
             both = jnp.concatenate([inners[:, s], d_weights.astype(BF16), no_rows], axis=0)
@@ -322,15 +326,6 @@
     d_radial = jnp.concatenate(d_radial, axis=1)
     d_envelope = jnp.concatenate(d_envelope, axis=1)
 
-    for l in range(2):
-        stacked_a[l * MULT : (l + 1) * MULT, :] = env_w[l]
-        stacked_b[l * MULT : (l + 1) * MULT, :] = stacked_a[(2 + l) * MULT : (3 + l) * MULT, :].astype(BF16)
-        stacked_b[(2 + l) * MULT : (3 + l) * MULT, :] = env_w[l].astype(BF16)
-    left = jnp.transpose(stacked_a[...], (1, 0)).astype(BF16)
-    d_products = (same[...] * dot(left, stacked_b[...])).astype(BF16)
-    d_y = dot(y_high, d_products)
-    d_way = [d_y[1 + c : 2 + c] for c in range(3)]
-
     slope_envelope = falling * scaled * (-4.0 / CUTOFF)
     d_envelope = d_envelope + jnp.sum(d_radial * over, axis=0, keepdims=True)
     d_over = d_radial * envelope
@@ -342,21 +337,10 @@
     )
     gradient = [d_way[c] * inverse + d_distance * way[c] for c in range(3)]
 
-    g8 = jnp.concatenate(gradient + [jnp.zeros((5, PAIRS), F32)], axis=0)
-    g_high = g8.astype(BF16).astype(F32)
-    g_low = g8 - g_high
     block_mask = rows_of((PADDED, PAIRS)) == block
     for c in range(3):
-        high, low = -g_high[c : c + 1], -g_low[c : c + 1]
-        spread = jnp.concatenate(
-            [
-                jnp.where(block_mask, high, 0.0).astype(BF16),
-                jnp.where(block_mask, low, 0.0).astype(BF16),
-            ],
-            axis=0,
-        )
-        both = dot_nt(spread, lane_neighbour[:BLK])
-        partial[:, c, :] = both[:ROWS] + both[PADDED : PADDED + ROWS]
+        spread = jnp.where(block_mask, -gradient[c], 0.0).astype(BF16)
+        partial[:, c, :] = dot_nt(spread, lane_neighbour[:BLK])[:ROWS]
     for offset in near:
         a, b, c = offset
         at = 9 * (a + 1) + 3 * (b + 1) + (c + 1)
@@ -369,19 +353,17 @@
             device_id_type=MESH,
         ).start()
     arrived[6 * 13 : 6 * 14] = partial[6 * 13 : 6 * 14]
-    own_mask = rows_of((8, PAIRS)) == centre_block
+    own_mask = rows_of((16, PAIRS)) == centre_block
     own_parts = []
     for c in range(3):
-        high, low = g_high[c : c + 1], g_low[c : c + 1]
-        spread = jnp.concatenate(
-            [
-                jnp.where(own_mask, high, 0.0),
-                jnp.where(own_mask, low, 0.0),
-            ],
-            axis=0,
-        ).astype(BF16)
-        both = dot_nt(spread, lane_centre[:BLK])
-        own_parts.append(both[:8] + both[8:])
+        spread = jnp.where(own_mask, gradient[c], 0.0).astype(BF16)
+        own_parts.append(dot_nt(spread, lane_centre[:BLK]))
+    energy = jnp.zeros((1, 1), F32)
+    for s in spans:
+        values = dot(out_row, latent[:, s].astype(BF16))
+        energy = energy + jnp.sum(values * live[:, s], axis=1, keepdims=True)
+    energy_ref[...] = jnp.broadcast_to(energy, (1, BLK))
+
     pltpu.make_async_copy(
         arrived.at[pl.ds(0, 6 * 26)], arrived.at[pl.ds(0, 6 * 26)], back_recv_sem
     ).wait()
@@ -402,6 +384,11 @@
     ).wait()
 
 
+def hand_over(forces_in, energy_in, forces_out, energy_out):
+    forces_out[...] = forces_in[...]
+    energy_out[0] = energy_in[0:1, 0:1]
+
+
 def on_device(sizes, positions, *arrays):
     *arrays, w_in, w_hidden, w_env, w_latent, w_out = arrays
     vmem = pltpu.VMEM
@@ -409,9 +396,11 @@
         functools.partial(kernel, sizes),
         out_shape=(
             jax.ShapeDtypeStruct((1, 1, 3, 1, 6 * BLK), F32),
-            jax.ShapeDtypeStruct((1, 1, 1), F32),
+            jax.ShapeDtypeStruct((1, BLK), F32),
         ),
-        in_specs=[pl.BlockSpec(memory_space=pltpu.HBM)] * 11,
+        in_specs=[pl.BlockSpec(memory_space=pltpu.HBM)] * 5
+        + [pl.BlockSpec(memory_space=pltpu.SMEM)]
+        + [pl.BlockSpec(memory_space=pltpu.HBM)] * 5,
         out_specs=(pl.BlockSpec(memory_space=vmem),) * 2,
         scratch_shapes=[
             vmem((3, 1, NB * BLK), F32),
@@ -446,6 +435,7 @@
             vmem((2, MULT, PAIRS), F32),
             vmem((4 * MULT, PAIRS), F32),
             vmem((4 * MULT, PAIRS), BF16),
+            vmem((PAIRS, 4 * MULT), BF16),
             vmem((6 * 27, 4, BLK), F32),
             vmem((6 * 27, 4, BLK), F32),
             pltpu.SemaphoreType.DMA((11,)),
@@ -467,6 +457,16 @@
         w_latent.transpose(0, 2, 1),
         w_out.reshape(2, CH // 2),
     )
+    forces, energy = pl.pallas_call(
+        hand_over,
+        out_shape=(
+            jax.ShapeDtypeStruct((1, 1, 3, 1, 6 * BLK), F32),
+            jax.ShapeDtypeStruct((1, 1, 1), F32),
+        ),
+        in_specs=(pl.BlockSpec(memory_space=vmem),) * 2,
+        out_specs=(pl.BlockSpec(memory_space=vmem),) * 2,
+        compiler_params=pltpu.CompilerParams(vmem_limit_bytes=63 * 1024 * 1024),
+    )(forces, energy)
     return forces.transpose(0, 1, 3, 2, 4), energy
 
 

time: 36.7 us -> 34.7 us (0.946)
  between operations: 3.05 us -> 1.29 us
  local copies, waits for them, and re-layouts: 1.3 us -> 0 us
  Pallas kernels: 32.1 us -> 33.2 us
    pallas_call x0 -> x1, Pallas kernels: none -> 1.31 us  [on_device(): pl.pallas_call(hand_over, out_shape=(jax.ShapeDtypeStruct((1, 1, 3, 1, 6...]
    unnamed x1 -> x0, local copies, waits for them, and re-layouts: 1.3 us -> none
where the time goes in v2:
time: 34.7 us; the launch traced here: 34.5 us
  Pallas kernels  33.2 us (96%)
  between operations  1.29 us (4%)
    pallas_call x1, Pallas kernels, on_device(): pl.pallas_call(functools.partial(kernel, sizes), out_shape=(jax.ShapeDtyp...  31.9 us
    pallas_call x1, Pallas kernels, on_device(): pl.pallas_call(hand_over, out_shape=(jax.ShapeDtypeStruct((1, 1, 3, 1, 6...  1.31 us

profile of v2, /device:TPU:1, one launch (start us, length us, event | category | flops | bytes accessed | tf_op | source)
XLA Modules:
  0.0 34.5 jit_solution(12029284417671631441)
XLA Ops:
  1.3 31.9 %shard_map.122 = (f32[1,1,3,1,768]{4,3,2,1,0:T(1,128)}, f32[1,128]{1,0:T(1,128)}) custom-call(f32[1,1,3,1,512]{4,3,2,1,0:T(1,128)} %bitcast.10, s32[1,1,1,512]{3,2,1,0:T(1,128)} %kind_hbm.1, s32[1,1,1,4]{3,2,1,0:T(1,128)} %plan_hbm.1, s32[1,1,1,512]{3,2,1,0:T(1,128)} %centre_hbm.1, s32[1,1,1,512]{3,2,1,0:T(1,128)} %neighbour_hbm.1, ...), custom_call_target="tpu_custom_call" | custom-call | flops 1000000000 | bytes 1000000 | tf_op jit(solution)/shard_map/pallas_call | solution.py:395
  33.2 1.3 %shard_map.123 = (f32[1,1,3,1,768]{4,3,2,1,0:T(1,128)}, f32[1,1,1]{2,1,0:T(1,128)}) custom-call(f32[1,1,3,1,768]{4,3,2,1,0:T(1,128)} %get-tuple-element.6.forces_in, f32[1,128]{1,0:T(1,128)} %get-tuple-element.7.energy_in), custom_call_target="tpu_custom_call" | custom-call | tf_op jit(solution)/shard_map/pallas_call | solution.py:460

commit v3 on v2

--- a/solution.py
+++ b/solution.py
@@ -27,7 +27,7 @@
 FIRST = {-2: 0, -1: 1, 0: 6, 1: 12, 2: 17}
 SENT = {-2: (5, 1), -1: (1, 5), 0: (0, 6), 1: (0, 5), 2: (0, 1)}
 ROWS = 9 * GROUP
-PADDED = 176
+PADDED = 164
 OWN = 4 * GROUP + FIRST[0]
 
 F32 = jnp.float32
@@ -145,6 +145,7 @@
             packed = packed + chosen * (mine[1 + b] + shift * first_row)
         mine[slot] = packed
     held[OWN : OWN + 6] = mine[...]
+    held[ROWS:] = jnp.zeros((PADDED - ROWS, 4, BLK), F32)
 
     pl.semaphore_wait(barrier, len(far))
     for offset in far:
@@ -219,21 +220,17 @@
         held.at[pl.ds(0, incoming)], held.at[pl.ds(0, incoming)], recv_sem
     ).wait()
 
-    neighbour_mask = rows_of((ROWS, PAIRS)) == neighbour_held
-    centre_mask = rows_of((GROUP, PAIRS)) == centre_held
-    near_rows = []
-    own_rows = []
-    for c in range(4):
-        table = held[:, c, :]
-        high, low = halves(table)
-        both = jnp.concatenate([high, low], axis=1)
-        found = dot(both, lane_neighbour[...])
-        near_rows.append(jnp.sum(jnp.where(neighbour_mask, found, 0.0), axis=0, keepdims=True))
-        table = held[4 * GROUP : 5 * GROUP, c, :]
-        high, low = halves(table)
-        both = jnp.concatenate([high, low], axis=1)
-        found = dot(both, lane_centre[...])
-        own_rows.append(jnp.sum(jnp.where(centre_mask, found, 0.0), axis=0, keepdims=True))
+    def found_at(table, hot, block_index):
+        count = table.shape[0] * 4
+        high, low = halves(table.reshape(count, BLK))
+        found = dot(jnp.concatenate([high, low], axis=1), hot)
+        found = jnp.where(rows_of((count, PAIRS)) >> 2 == block_index, found, 0.0)
+        found = jnp.sum(found.reshape(count // 8, 8, PAIRS), axis=0)
+        found = found[0:4] + found[4:8]
+        return [found[c : c + 1] for c in range(4)]
+
+    near_rows = found_at(held[...], lane_neighbour[...], neighbour_held)
+    own_rows = found_at(held[4 * GROUP : 4 * GROUP + 20], lane_centre[...], centre_held)
 
     shifts = [EDGE * (v.astype(F32) - 1.0) for v in (box_x, box_y, box_z)]
     gap = [near_rows[c] + shifts[c] - own_rows[c] for c in range(3)]
@@ -337,10 +334,14 @@
     )
     gradient = [d_way[c] * inverse + d_distance * way[c] for c in range(3)]
 
-    block_mask = rows_of((PADDED, PAIRS)) == block
-    for c in range(3):
-        spread = jnp.where(block_mask, -gradient[c], 0.0).astype(BF16)
-        partial[:, c, :] = dot_nt(spread, lane_neighbour[:BLK])[:ROWS]
+    def scattered(count, values, hot, block_index):
+        pattern = jnp.concatenate(values + [jnp.zeros((1, PAIRS), F32)], axis=0)
+        pattern = jnp.concatenate([pattern, pattern], axis=0)
+        pattern = jnp.broadcast_to(pattern[None], (count // 2, 8, PAIRS)).reshape(4 * count, PAIRS)
+        spread = jnp.where(rows_of((4 * count, PAIRS)) >> 2 == block_index, pattern, 0.0)
+        return dot_nt(spread.astype(BF16), hot).reshape(count, 4, BLK)
+
+    partial[...] = scattered(PADDED, [-g for g in gradient], lane_neighbour[:BLK], block)
     for offset in near:
         a, b, c = offset
         at = 9 * (a + 1) + 3 * (b + 1) + (c + 1)
@@ -353,11 +354,7 @@
             device_id_type=MESH,
         ).start()
     arrived[6 * 13 : 6 * 14] = partial[6 * 13 : 6 * 14]
-    own_mask = rows_of((16, PAIRS)) == centre_block
-    own_parts = []
-    for c in range(3):
-        spread = jnp.where(own_mask, gradient[c], 0.0).astype(BF16)
-        own_parts.append(dot_nt(spread, lane_centre[:BLK]))
+    own_part = scattered(8, gradient, lane_centre[:BLK], centre_block)
     energy = jnp.zeros((1, 1), F32)
     for s in spans:
         values = dot(out_row, latent[:, s].astype(BF16))
@@ -368,13 +365,11 @@
         arrived.at[pl.ds(0, 6 * 26)], arrived.at[pl.ds(0, 6 * 26)], back_recv_sem
     ).wait()
     for s in range(6):
-        total = arrived[s]
-        for o in range(1, 27):
+        total = own_part[s]
+        for o in range(27):
             total = total + arrived[6 * o + s]
         for c in range(3):
-            forces_ref[0, 0, c, :, s * BLK : (s + 1) * BLK] = (
-                total[c : c + 1] + own_parts[c][s : s + 1]
-            )
+            forces_ref[0, 0, c, :, s * BLK : (s + 1) * BLK] = total[c : c + 1]
 
     pltpu.make_async_copy(
         held.at[pl.ds(0, incoming)], held.at[pl.ds(0, incoming)], send_sem
@@ -420,7 +415,7 @@
             vmem((2, CH, CH + BLK), BF16),
             vmem((2, CH, CH + BLK), BF16),
             vmem((6, 4, BLK), F32),
-            vmem((ROWS, 4, BLK), F32),
+            vmem((PADDED, 4, BLK), F32),
             vmem((2 * BLK, PAIRS), BF16),
             vmem((2 * BLK, PAIRS), BF16),
             vmem((PAIRS, PAIRS), F32),
@@ -436,7 +431,7 @@
             vmem((4 * MULT, PAIRS), F32),
             vmem((4 * MULT, PAIRS), BF16),
             vmem((PAIRS, 4 * MULT), BF16),
-            vmem((6 * 27, 4, BLK), F32),
+            vmem((PADDED, 4, BLK), F32),
             vmem((6 * 27, 4, BLK), F32),
             pltpu.SemaphoreType.DMA((11,)),
             pltpu.SemaphoreType.DMA,

time: 34.7 us -> 33.8 us (0.974)
  Pallas kernels: 33.2 us -> 32.3 us
    pallas_call x1, Pallas kernels: 31.9 us -> 31 us  [on_device(): pl.pallas_call(functools.partial(kernel, sizes), out_shape=(jax.ShapeDtyp...]
where the time goes in v3:
time: 33.8 us; the launch traced here: 33.6 us
  Pallas kernels  32.3 us (96%)
  between operations  1.29 us (4%)
    pallas_call x1, Pallas kernels, on_device(): pl.pallas_call(functools.partial(kernel, sizes), out_shape=(jax.ShapeDtyp...  31 us
    pallas_call x1, Pallas kernels, on_device(): pl.pallas_call(hand_over, out_shape=(jax.ShapeDtypeStruct((1, 1, 3, 1, 6...  1.31 us

profile of v3, /device:TPU:1, one launch (start us, length us, event | category | flops | bytes accessed | tf_op | source)
XLA Modules:
  0.0 33.6 jit_solution(6642118552560203164)
XLA Ops:
  1.3 31.0 %shard_map.122 = (f32[1,1,3,1,768]{4,3,2,1,0:T(1,128)}, f32[1,128]{1,0:T(1,128)}) custom-call(f32[1,1,3,1,512]{4,3,2,1,0:T(1,128)} %bitcast.10, s32[1,1,1,512]{3,2,1,0:T(1,128)} %kind_hbm.1, s32[1,1,1,4]{3,2,1,0:T(1,128)} %plan_hbm.1, s32[1,1,1,512]{3,2,1,0:T(1,128)} %centre_hbm.1, s32[1,1,1,512]{3,2,1,0:T(1,128)} %neighbour_hbm.1, ...), custom_call_target="tpu_custom_call" | custom-call | flops 1000000000 | bytes 1000000 | tf_op jit(solution)/shard_map/pallas_call | solution.py:390
  32.3 1.3 %shard_map.123 = (f32[1,1,3,1,768]{4,3,2,1,0:T(1,128)}, f32[1,1,1]{2,1,0:T(1,128)}) custom-call(f32[1,1,3,1,768]{4,3,2,1,0:T(1,128)} %get-tuple-element.6.forces_in, f32[1,128]{1,0:T(1,128)} %get-tuple-element.7.energy_in), custom_call_target="tpu_custom_call" | custom-call | tf_op jit(solution)/shard_map/pallas_call | solution.py:455

commit v4 on v3

--- a/solution.py
+++ b/solution.py
@@ -84,7 +84,7 @@
     sizes,
     pos_hbm, kind_hbm, plan_hbm, centre_hbm, neighbour_hbm, blocks_hbm,
     w_in_hbm, w_hidden_hbm, w_env_hbm, w_latent_hbm, w_out_hbm,
-    forces_ref, energy_ref,
+    results,
     pos, kind, plan, centre, neighbour, blocks,
     w_in_raw, w_hidden, w_env, w_latent_t, w_out,
     w_in_t, w_in, w_hidden_t, w_back, w_latent,
@@ -103,7 +103,8 @@
 
     far = [(a, b, c) for b in (-1, 0, 1) for c in (-1, 0, 1) for a in (-2, -1, 0, 1, 2)]
     far = [o for o in far if o != (0, 0, 0)]
-    far.sort(key=lambda o: -(abs(o[0]) + abs(o[1]) + abs(o[2])))
+    far.sort(key=lambda o: -(2 * (abs(o[1]) + abs(o[2])) + abs(o[0])))
+    far = [x for o in far if o > (0, 0, 0) for x in (o, (-o[0], -o[1], -o[2]))]
     near = [o for o in far if abs(o[0]) < 2]
 
     pairs_in = [
@@ -268,7 +269,6 @@
 
     spans = [slice(j * CHUNK, (j + 1) * CHUNK) for j in range(CHUNKS)]
 
-    before = []
     for s in spans:
         value, slope = silu_parts(dot(w_in[...], features[:, s]))
         d1[:, s] = slope
@@ -280,13 +280,15 @@
         for j, s in enumerate(spans):
             half = latent[:, s].astype(BF16)
             env_w[l, :, s] = dot(w_env[l], half) * live[:, s]
-            dz[l, :, s] = dot(w_latent[l, :, :CH], half)
+            inners[:, s] = half
         weights_half = env_w[l].astype(BF16)
         for j, s in enumerate(spans):
             gathered = dot(weights_half, g_matrix[:, s])
             env_a[l, :, s] = gathered
             invariant = (0.5 * env_w[l, :, s] * gathered).astype(BF16)
-            value, slope = silu_parts(dz[l, :, s] + dot(w_latent[l, :, CH:], jnp.concatenate([invariant, no_rows], axis=0)))
+            value, slope = silu_parts(
+                dot(w_latent[l], jnp.concatenate([inners[:, s], invariant, no_rows], axis=0))
+            )
             dz[l, :, s] = slope
             latent[:, s] = latent[:, s] + value
     for l in range(2):
@@ -359,7 +361,7 @@
     for s in spans:
         values = dot(out_row, latent[:, s].astype(BF16))
         energy = energy + jnp.sum(values * live[:, s], axis=1, keepdims=True)
-    energy_ref[...] = jnp.broadcast_to(energy, (1, BLK))
+    results[0, 0, 3, :, :BLK] = jnp.broadcast_to(energy, (1, BLK))
 
     pltpu.make_async_copy(
         arrived.at[pl.ds(0, 6 * 26)], arrived.at[pl.ds(0, 6 * 26)], back_recv_sem
@@ -369,7 +371,9 @@
         for o in range(27):
             total = total + arrived[6 * o + s]
         for c in range(3):
-            forces_ref[0, 0, c, :, s * BLK : (s + 1) * BLK] = total[c : c + 1]
+            results[0, 0, c, :, s * BLK : (s + 1) * BLK] = total[c : c + 1]
+
+    results[0, 0, 3, :, BLK:] = jnp.zeros((1, 5 * BLK), F32)
 
     pltpu.make_async_copy(
         held.at[pl.ds(0, incoming)], held.at[pl.ds(0, incoming)], send_sem
@@ -379,24 +383,21 @@
     ).wait()
 
 
-def hand_over(forces_in, energy_in, forces_out, energy_out):
-    forces_out[...] = forces_in[...]
-    energy_out[0] = energy_in[0:1, 0:1]
+def hand_over(results, forces, energy):
+    forces[...] = results[:, :, :3]
+    energy[0] = results[0, 0, 3, :, 0:1]
 
 
 def on_device(sizes, positions, *arrays):
     *arrays, w_in, w_hidden, w_env, w_latent, w_out = arrays
     vmem = pltpu.VMEM
-    forces, energy = pl.pallas_call(
+    results = pl.pallas_call(
         functools.partial(kernel, sizes),
-        out_shape=(
-            jax.ShapeDtypeStruct((1, 1, 3, 1, 6 * BLK), F32),
-            jax.ShapeDtypeStruct((1, BLK), F32),
-        ),
+        out_shape=jax.ShapeDtypeStruct((1, 1, 4, 1, 6 * BLK), F32),
         in_specs=[pl.BlockSpec(memory_space=pltpu.HBM)] * 5
         + [pl.BlockSpec(memory_space=pltpu.SMEM)]
         + [pl.BlockSpec(memory_space=pltpu.HBM)] * 5,
-        out_specs=(pl.BlockSpec(memory_space=vmem),) * 2,
+        out_specs=pl.BlockSpec(memory_space=vmem),
         scratch_shapes=[
             vmem((3, 1, NB * BLK), F32),
             vmem((1, NB * BLK), jnp.int32),
@@ -458,10 +459,10 @@
             jax.ShapeDtypeStruct((1, 1, 3, 1, 6 * BLK), F32),
             jax.ShapeDtypeStruct((1, 1, 1), F32),
         ),
-        in_specs=(pl.BlockSpec(memory_space=vmem),) * 2,
+        in_specs=(pl.BlockSpec(memory_space=vmem),),
         out_specs=(pl.BlockSpec(memory_space=vmem),) * 2,
         compiler_params=pltpu.CompilerParams(vmem_limit_bytes=63 * 1024 * 1024),
-    )(forces, energy)
+    )(results)
     return forces.transpose(0, 1, 3, 2, 4), energy
 
 

time: 33.8 us -> 33.3 us (0.985)
  Pallas kernels: 32.3 us -> 31.8 us
    pallas_call x1, Pallas kernels: 31 us -> 30.4 us  [on_device(): pl.pallas_call(functools.partial(kernel, sizes), out_shape=jax.ShapeDtype...]
where the time goes in v4:
time: 33.3 us; the launch traced here: 33 us
  Pallas kernels  31.8 us (95%)
  between operations  1.29 us (4%)
    pallas_call x1, Pallas kernels, on_device(): pl.pallas_call(functools.partial(kernel, sizes), out_shape=jax.ShapeDtype...  30.4 us
    pallas_call x1, Pallas kernels, on_device(): pl.pallas_call(hand_over, out_shape=(jax.ShapeDtypeStruct((1, 1, 3, 1, 6...  1.31 us

profile of v4, /device:TPU:1, one launch (start us, length us, event | category | flops | bytes accessed | tf_op | source)
XLA Modules:
  0.0 33.0 jit_solution(2473244281321072499)
XLA Ops:
  1.3 30.4 %shard_map.122.results = f32[1,1,4,1,768]{4,3,2,1,0:T(1,128)} custom-call(f32[1,1,3,1,512]{4,3,2,1,0:T(1,128)} %bitcast.10, s32[1,1,1,512]{3,2,1,0:T(1,128)} %kind_hbm.1, s32[1,1,1,4]{3,2,1,0:T(1,128)} %plan_hbm.1, s32[1,1,1,512]{3,2,1,0:T(1,128)} %centre_hbm.1, s32[1,1,1,512]{3,2,1,0:T(1,128)} %neighbour_hbm.1, s32[1,1,1]{2,1,0:T(1,128)S(6)} %copy.14.blocks_hbm, ...), custom_call_target="tpu_custom_call" | custom-call | flops 1000000000 | bytes 1000000 | tf_op jit(solution)/shard_map/pallas_call | solution.py:394
  31.7 1.3 %shard_map.123 = (f32[1,1,3,1,768]{4,3,2,1,0:T(1,128)}, f32[1,1,1]{2,1,0:T(1,128)}) custom-call(f32[1,1,4,1,768]{4,3,2,1,0:T(1,128)} %shard_map.122.results), custom_call_target="tpu_custom_call" | custom-call | tf_op jit(solution)/shard_map/pallas_call | solution.py:456

commit v5 on v4

--- a/solution.py
+++ b/solution.py
@@ -187,6 +187,10 @@
 
     neighbour_held = held_row(box_x, box_yz, k)
     centre_held = held_row(jnp.ones_like(centre_block), jnp.zeros_like(centre_block), centre_block)
+    home = jnp.zeros_like(box)
+    for at, (a, b, c) in enumerate(near + [(0, 0, 0)]):
+        home = home + jnp.where(box == 9 * (a + 1) + 3 * (b + 1) + (c + 1), at, 0)
+    neighbour_home = 6 * home + k
     lanes = rows_of((BLK, PAIRS))
     hot = jnp.where(lanes == neighbour_lane, 1.0, 0.0).astype(BF16)
     lane_neighbour[:BLK] = hot
@@ -343,19 +347,27 @@
         spread = jnp.where(rows_of((4 * count, PAIRS)) >> 2 == block_index, pattern, 0.0)
         return dot_nt(spread.astype(BF16), hot).reshape(count, 4, BLK)
 
-    partial[...] = scattered(PADDED, [-g for g in gradient], lane_neighbour[:BLK], block)
-    for offset in near:
-        a, b, c = offset
-        at = 9 * (a + 1) + 3 * (b + 1) + (c + 1)
-        pltpu.make_async_remote_copy(
-            src_ref=partial.at[pl.ds(6 * at, 6)],
-            dst_ref=arrived.at[pl.ds(6 * at, 6)],
-            send_sem=back_send_sem,
-            recv_sem=back_recv_sem,
-            device_id=device(offset),
-            device_id_type=MESH,
-        ).start()
-    arrived[6 * 13 : 6 * 14] = partial[6 * 13 : 6 * 14]
+    def send_back(places):
+        for at in places:
+            offset = near[at]
+            pltpu.make_async_remote_copy(
+                src_ref=partial.at[pl.ds(6 * at, 6)],
+                dst_ref=arrived.at[pl.ds(6 * at, 6)],
+                send_sem=back_send_sem,
+                recv_sem=back_recv_sem,
+                device_id=device(offset),
+                device_id_type=MESH,
+            ).start()
+
+    negative = [-g for g in gradient]
+    for first, last in ((0, 14), (14, 27)):
+        count = 6 * (last - first)
+        padded = count + count % 4
+        partial[6 * first : 6 * first + padded] = scattered(
+            padded, negative, lane_neighbour[:BLK], neighbour_home - 6 * first
+        )
+        send_back(range(first, min(last, 26)))
+    arrived[6 * 26 : 6 * 27] = partial[6 * 26 : 6 * 27]
     own_part = scattered(8, gradient, lane_centre[:BLK], centre_block)
     energy = jnp.zeros((1, 1), F32)
     for s in spans:

time: 33.3 us -> 33.2 us (level)
  no operation moved by 1% of the time
where the time goes in v5:
time: 33.2 us; the launch traced here: 32.9 us
  Pallas kernels  31.7 us (95%)
  between operations  1.29 us (4%)
    pallas_call x1, Pallas kernels, on_device(): pl.pallas_call(functools.partial(kernel, sizes), out_shape=jax.ShapeDtype...  30.4 us
    pallas_call x1, Pallas kernels, on_device(): pl.pallas_call(hand_over, out_shape=(jax.ShapeDtypeStruct((1, 1, 3, 1, 6...  1.31 us

profile of v5, /device:TPU:1, one launch (start us, length us, event | category | flops | bytes accessed | tf_op | source)
XLA Modules:
  0.0 32.9 jit_solution(14975747001875520632)
XLA Ops:
  1.3 30.4 %shard_map.122.results = f32[1,1,4,1,768]{4,3,2,1,0:T(1,128)} custom-call(f32[1,1,3,1,512]{4,3,2,1,0:T(1,128)} %bitcast.10, s32[1,1,1,512]{3,2,1,0:T(1,128)} %kind_hbm.1, s32[1,1,1,4]{3,2,1,0:T(1,128)} %plan_hbm.1, s32[1,1,1,512]{3,2,1,0:T(1,128)} %centre_hbm.1, s32[1,1,1,512]{3,2,1,0:T(1,128)} %neighbour_hbm.1, s32[1,1,1]{2,1,0:T(1,128)S(6)} %copy.14.blocks_hbm, ...), custom_call_target="tpu_custom_call" | custom-call | flops 1000000000 | bytes 1000000 | tf_op jit(solution)/shard_map/pallas_call | solution.py:406
  31.6 1.3 %shard_map.123 = (f32[1,1,3,1,768]{4,3,2,1,0:T(1,128)}, f32[1,1,1]{2,1,0:T(1,128)}) custom-call(f32[1,1,4,1,768]{4,3,2,1,0:T(1,128)} %shard_map.122.results), custom_call_target="tpu_custom_call" | custom-call | tf_op jit(solution)/shard_map/pallas_call | solution.py:468
